TPU v7x, 32 devices: a whole 2x2x4 slice. The times are simulated.
32 devices in a mesh: head: 4 (over z), ctx: 8 (over y, x, core).
Axes of the slice: x: 2, y: 2, z: 4, core: 2. Of those that a mesh axis runs over, the one named last changes fastest.
Arguments:
- queries: bfloat16 [2048, 3584], P(('head', 'ctx')), may hold values from -6 to 6
- keys: bfloat16 [2048, 512], P(('head', 'ctx')), may hold values from -12 to 12
- values: bfloat16 [2048, 512], P(('head', 'ctx')), may hold values from -6 to 6
- block_index: int32 [16, 28, 16], replicated, may hold values from 0 to 15, as said below
- block_count: int32 [16, 28], replicated, may hold values from 1 to 16, as said below
- head_order: int32 [28], replicated, may hold values from 0 to 27, as said below
Outputs:
- attention_out: bfloat16 [2048, 3584], P(('head', 'ctx'))
Inputs may be any that keep to these rules, and one draw needn't show every extreme that they name: For query block b and head h the first block_count[b, h] entries of block_index[b, h] are distinct key blocks in ascending order, always including block 0 and block b and never above b; the later entries name the remaining blocks. block_count[b, h] is at most b + 1. `head_order`: A permutation of the 28 query heads; each aligned block of 7 entries that starts at a multiple of 7 holds heads of exactly two key and value heads (head // 7).
All inputs are finite; a program needn't handle non-finite values.
Results may differ from a plain program's by a relative error of at most 0.0045.
Values may be sent and summed in bfloat16 or wider, within the bound.
A program may use at most 64 MiB of HBM per device.

v0:
```python
from functools import partial
import math

import jax
import jax.numpy as jnp
from jax import lax
from jax.sharding import PartitionSpec as P

H = 28
KVH = 4
HD = 128
BLOCK = 128


FLOOR = -1e30


def positions(stripes, stripe_len, device, ctx_total):
    offsets = jnp.arange(stripes * stripe_len, dtype=jnp.int32)
    stripe = offsets // stripe_len
    return (stripe * ctx_total + device) * stripe_len + offsets % stripe_len


def keep_state(carried):
    return carried


def update_lanes(query_rows, key_lanes, value_lanes, allowed, score_scale, carried):
    running_max, running_sum, running_out = carried
    scores = (
        jnp.einsum("qgd,kgd->qgk", query_rows, key_lanes, preferred_element_type=jnp.float32)
        * score_scale
    )
    scores = jnp.where(allowed, scores, FLOOR)
    new_max = jnp.maximum(running_max, jnp.max(scores, axis=2))
    weights = jnp.where(allowed, jnp.exp(scores - new_max[:, :, None]), 0.0)
    factor = jnp.exp(running_max - new_max)
    new_sum = running_sum * factor + jnp.sum(weights, axis=2)
    update = jnp.einsum(
        "qgk,kgd->qgd",
        weights.astype(jnp.bfloat16),
        value_lanes,
        preferred_element_type=jnp.float32,
    )
    new_out = running_out * factor[:, :, None] + update
    return (new_max, new_sum, new_out)


def local(queries, keys, values, block_index, block_count, head_order):
    local_tokens = queries.shape[0]
    per_group = H // KVH
    head_total = lax.axis_size("head")
    ctx_total = lax.axis_size("ctx")
    ctx_here = lax.axis_index("ctx")
    head_here = lax.axis_index("head")
    query_split = queries.reshape(local_tokens, H, HD)
    key_split = keys.reshape(local_tokens, KVH, HD)
    value_split = values.reshape(local_tokens, KVH, HD)
    query_sorted = jnp.take(query_split, head_order, axis=1)
    kv_lists = (head_order // per_group).reshape(head_total, per_group)
    kv_pairs = jnp.stack([jnp.min(kv_lists, axis=1), jnp.max(kv_lists, axis=1)], axis=1).reshape(
        head_total * 2
    )
    key_sent = jnp.take(key_split, kv_pairs, axis=1).reshape(local_tokens, head_total, 2, HD)
    value_sent = jnp.take(value_split, kv_pairs, axis=1).reshape(local_tokens, head_total, 2, HD)
    own_heads = lax.dynamic_slice_in_dim(head_order, head_here * per_group, per_group)
    own_kv = own_heads // per_group
    slot_of = (own_kv == jnp.max(own_kv)).astype(jnp.int32)
    query_sent = query_sorted.reshape(local_tokens, head_total, per_group, HD)
    query_got, key_got, value_got = (
        lax.all_to_all(query_sent, "head", split_axis=1, concat_axis=0, tiled=True),
        lax.all_to_all(key_sent, "head", split_axis=1, concat_axis=0, tiled=True),
        lax.all_to_all(value_sent, "head", split_axis=1, concat_axis=0, tiled=True),
    )
    row_count = head_total * local_tokens
    slot_count = key_sent.shape[2]
    query_rows = query_got.reshape(row_count, per_group, HD)
    key_rows = key_got.reshape(row_count, slot_count, HD)
    value_rows = value_got.reshape(row_count, slot_count, HD)
    query_pos = positions(head_total, local_tokens, ctx_here, ctx_total)
    per_entry = min(local_tokens, BLOCK)
    entries = row_count // per_entry
    entry_blocks = query_pos[::per_entry] // BLOCK
    block_total = block_index.shape[2]
    block_iota = jnp.arange(block_total, dtype=jnp.int32)
    listed = jnp.take(jnp.take(block_index, entry_blocks, axis=0), own_heads, axis=1)
    counted = jnp.take(jnp.take(block_count, entry_blocks, axis=0), own_heads, axis=1)
    usable = block_iota[None, None, :] < counted[:, :, None]
    block_hits = (listed[:, :, :, None] == block_iota[None, None, None, :]) & usable[:, :, :, None]
    table_flags = jnp.any(block_hits, axis=2).astype(jnp.bfloat16)
    score_scale = 1.0 / math.sqrt(HD)
    initial = (
        jnp.full((row_count, per_group), FLOOR, jnp.float32),
        jnp.zeros((row_count, per_group), jnp.float32),
        jnp.zeros((row_count, per_group, HD), jnp.float32),
    )
    key_piece = lax.all_gather(key_rows, "ctx", axis=0, tiled=True)
    value_piece = lax.all_gather(value_rows, "ctx", axis=0, tiled=True)
    shard_total = key_piece.shape[0] // row_count

    def one_shard(number, inner_state):
        key_block = lax.dynamic_slice_in_dim(key_piece, number * row_count, row_count, 0)
        value_block = lax.dynamic_slice_in_dim(value_piece, number * row_count, row_count, 0)
        key_lanes = jnp.take(key_block, slot_of, axis=1)
        value_lanes = jnp.take(value_block, slot_of, axis=1)
        key_pos = positions(head_total, local_tokens, number, ctx_total)
        onehot = (block_iota[:, None] == (key_pos // BLOCK)[None, :]).astype(jnp.bfloat16)
        chosen = jnp.einsum("egb,bk->egk", table_flags, onehot, preferred_element_type=jnp.float32)
        spread = jnp.broadcast_to(
            chosen[:, None], (entries, per_entry, per_group, row_count)
        ).reshape(row_count, per_group, row_count)
        allowed = (spread > 0.5) & (key_pos[None, None, :] <= query_pos[:, None, None])
        return lax.cond(
            jnp.any(allowed),
            partial(update_lanes, query_rows, key_lanes, value_lanes, allowed, score_scale),
            keep_state,
            inner_state,
        )

    folded = lax.fori_loop(0, shard_total, one_shard, initial)
    running_max, running_sum, running_out = folded
    attended = (
        (running_out / running_sum[:, :, None])
        .astype(jnp.bfloat16)
        .reshape(row_count, 1, per_group, HD)
    )
    returned = lax.all_to_all(attended, "head", split_axis=0, concat_axis=1, tiled=True).reshape(
        local_tokens, H, HD
    )
    return returned.reshape(local_tokens, H * HD)


def solution(mesh):
    return jax.shard_map(
        local,
        mesh=mesh,
        in_specs=(
            P(("head", "ctx"), None),
            P(("head", "ctx"), None),
            P(("head", "ctx"), None),
            P(),
            P(),
            P(),
        ),
        out_specs=P(("head", "ctx"), None),
        check_vma=False,
    )
```

profile of v0, /device:TPU:0, one launch (start us, length us, event | category | flops | bytes accessed | tf_op | source)
XLA Modules:
  0.0 163.3 jit_solution(13714687349221478223)
XLA Ops:
  11.4 12.2 %all_to_all.60 = bf16[64,4,2,128]{3,0,2,1:T(8,128)(2,1)S(1)} all-to-all(bf16[64,4,2,128]{3,0,2,1:T(8,128)(2,1)S(1)} %bitcast.93), channel_id=1, replica_groups=mesh['head'=4,'ctx'=8] {'head'}, dimensions={1} | all-to-all | bytes 262144 | tf_op jit(solution)/shard_map/all_to_all | solution.py:72
  24.2 3.3 %all-to-all-start.1 = ((bf16[64,4,2,128]{3,0,2,1:T(8,128)(2,1)}), bf16[64,4,2,128]{3,0,2,1:T(8,128)(2,1)S(1)}, u32[]{:S(2)}, u32[]{:S(2)}) async-start(bf16[64,4,2,128]{3,0,2,1:T(8,128)(2,1)} %bitcast.13), calls=%async_computation.1 | async-start | bytes 262144 | tf_op jit(solution)/shard_map/all_to_all | solution.py:73
  29.5 4.0 %all-to-all-done.1 = bf16[64,4,2,128]{3,0,2,1:T(8,128)(2,1)S(1)} async-done(((bf16[64,4,2,128]{3,0,2,1:T(8,128)(2,1)}), bf16[64,4,2,128]{3,0,2,1:T(8,128)(2,1)S(1)}, u32[]{:S(2)}, u32[]{:S(2)}) %all-to-all-start.1) | async-done | bytes 131104 | tf_op jit(solution)/shard_map/all_to_all | solution.py:73
  33.5 3.5 %all-to-all-start.2 = ((bf16[64,4,7,128]{3,0,2,1:T(8,128)(2,1)}), bf16[64,4,7,128]{3,0,2,1:T(8,128)(2,1)S(1)}, u32[]{:S(2)}, u32[]{:S(2)}) async-start(bf16[64,4,7,128]{3,0,2,1:T(8,128)(2,1)} %broadcast_select_fusion), calls=%async_computation.2 | async-start | bytes 917504 | tf_op jit(solution)/shard_map/all_to_all | solution.py:71
  42.4 5.3 %all-to-all-done.2 = bf16[64,4,7,128]{3,0,2,1:T(8,128)(2,1)S(1)} async-done(((bf16[64,4,7,128]{3,0,2,1:T(8,128)(2,1)}), bf16[64,4,7,128]{3,0,2,1:T(8,128)(2,1)S(1)}, u32[]{:S(2)}, u32[]{:S(2)}) %all-to-all-start.2) | async-done | bytes 458784 | tf_op jit(solution)/shard_map/all_to_all | solution.py:71
  47.8 24.7 %all-gather.5.cloned.1.call-done = bf16[2048,2,128]{2,0,1:T(8,128)(2,1)} async-done(((bf16[256,2,128]{2,0,1:T(8,128)(2,1)}), bf16[2048,2,128]{2,0,1:T(8,128)(2,1)}) %all-gather.5.cloned.1.call-update) | async-done | bytes 1048592 | tf_op jit(solution)/shard_map/all_gather | solution.py:98
  72.5 62.5 %while.21 = (s32[]{:T(128)}, f32[256,7]{0,1:T(8,128)S(1)}, f32[256,7]{0,1:T(8,128)S(1)}, f32[256,7,128]{2,0,1:T(8,128)S(1)}, bf16[4,7,16]{2,1,0:T(8,128)(2,1)S(1...) while((s32[]{:T(128)}, f32[256,7]{0,1:T(8,128)S(1)}, ...), condition=%wide.region_10.13_spmd.clone, body=%wide.region_4.0_spmd.clone.sunk | while | flops 244452416 | bytes 16272775 | solution.py:120
  72.9 1.1 and_reduce_fusion.2
  77.1 3.2 %conditional.3 = ((f32[256,7]{0,1:T(8,128)S(1)}, f32[256,7]{0,1:T(8,128)S(1)}, f32[256,7,128]{2,0,1:T(8,128)S(1)})) conditional(s32[]{:T(128)} %convert_element_type.37, (f32[256,7]{0,1:T(8,128)S(1)}, f32[256,7]{0,1:T(8,128)S(1)}, f32[256,7,128]{2,0,1:T(8,128)S(1)}) %tuple.80, (f32[4,7,256]{2,1,0:T(8,128)S(1)}, s32[256]{0:T(256)S(1)}, ...), branch_computations={%region_6.8_spmd, %region_7.11_spmd} | conditional | flops 242756096 | bytes 11890720 | solution.py:113
  79.1 1.1 fusion.5
  80.7 1.1 and_reduce_fusion.2
  84.9 3.2 %conditional.3 = ((f32[256,7]{0,1:T(8,128)S(1)}, f32[256,7]{0,1:T(8,128)S(1)}, f32[256,7,128]{2,0,1:T(8,128)S(1)})) conditional(s32[]{:T(128)} %convert_element_type.37, (f32[256,7]{0,1:T(8,128)S(1)}, f32[256,7]{0,1:T(8,128)S(1)}, f32[256,7,128]{2,0,1:T(8,128)S(1)}) %tuple.80, (f32[4,7,256]{2,1,0:T(8,128)S(1)}, s32[256]{0:T(256)S(1)}, ...), branch_computations={%region_6.8_spmd, %region_7.11_spmd} | conditional | flops 242756096 | bytes 11890720 | solution.py:113
  87.0 1.1 fusion.5
  88.5 1.1 and_reduce_fusion.2
  92.7 3.2 %conditional.3 = ((f32[256,7]{0,1:T(8,128)S(1)}, f32[256,7]{0,1:T(8,128)S(1)}, f32[256,7,128]{2,0,1:T(8,128)S(1)})) conditional(s32[]{:T(128)} %convert_element_type.37, (f32[256,7]{0,1:T(8,128)S(1)}, f32[256,7]{0,1:T(8,128)S(1)}, f32[256,7,128]{2,0,1:T(8,128)S(1)}) %tuple.80, (f32[4,7,256]{2,1,0:T(8,128)S(1)}, s32[256]{0:T(256)S(1)}, ...), branch_computations={%region_6.8_spmd, %region_7.11_spmd} | conditional | flops 242756096 | bytes 11890720 | solution.py:113
  94.8 1.1 fusion.5
  96.3 1.1 and_reduce_fusion.2
  100.5 3.2 %conditional.3 = ((f32[256,7]{0,1:T(8,128)S(1)}, f32[256,7]{0,1:T(8,128)S(1)}, f32[256,7,128]{2,0,1:T(8,128)S(1)})) conditional(s32[]{:T(128)} %convert_element_type.37, (f32[256,7]{0,1:T(8,128)S(1)}, f32[256,7]{0,1:T(8,128)S(1)}, f32[256,7,128]{2,0,1:T(8,128)S(1)}) %tuple.80, (f32[4,7,256]{2,1,0:T(8,128)S(1)}, s32[256]{0:T(256)S(1)}, ...), branch_computations={%region_6.8_spmd, %region_7.11_spmd} | conditional | flops 242756096 | bytes 11890720 | solution.py:113
  102.6 1.1 fusion.5
  104.1 1.1 and_reduce_fusion.2
  108.4 3.2 %conditional.3 = ((f32[256,7]{0,1:T(8,128)S(1)}, f32[256,7]{0,1:T(8,128)S(1)}, f32[256,7,128]{2,0,1:T(8,128)S(1)})) conditional(s32[]{:T(128)} %convert_element_type.37, (f32[256,7]{0,1:T(8,128)S(1)}, f32[256,7]{0,1:T(8,128)S(1)}, f32[256,7,128]{2,0,1:T(8,128)S(1)}) %tuple.80, (f32[4,7,256]{2,1,0:T(8,128)S(1)}, s32[256]{0:T(256)S(1)}, ...), branch_computations={%region_6.8_spmd, %region_7.11_spmd} | conditional | flops 242756096 | bytes 11890720 | solution.py:113
  110.4 1.1 fusion.5
  112.0 1.1 and_reduce_fusion.2
  116.2 3.2 %conditional.3 = ((f32[256,7]{0,1:T(8,128)S(1)}, f32[256,7]{0,1:T(8,128)S(1)}, f32[256,7,128]{2,0,1:T(8,128)S(1)})) conditional(s32[]{:T(128)} %convert_element_type.37, (f32[256,7]{0,1:T(8,128)S(1)}, f32[256,7]{0,1:T(8,128)S(1)}, f32[256,7,128]{2,0,1:T(8,128)S(1)}) %tuple.80, (f32[4,7,256]{2,1,0:T(8,128)S(1)}, s32[256]{0:T(256)S(1)}, ...), branch_computations={%region_6.8_spmd, %region_7.11_spmd} | conditional | flops 242756096 | bytes 11890720 | solution.py:113
  118.2 1.1 fusion.5
  119.8 1.1 and_reduce_fusion.2
  124.0 3.2 %conditional.3 = ((f32[256,7]{0,1:T(8,128)S(1)}, f32[256,7]{0,1:T(8,128)S(1)}, f32[256,7,128]{2,0,1:T(8,128)S(1)})) conditional(s32[]{:T(128)} %convert_element_type.37, (f32[256,7]{0,1:T(8,128)S(1)}, f32[256,7]{0,1:T(8,128)S(1)}, f32[256,7,128]{2,0,1:T(8,128)S(1)}) %tuple.80, (f32[4,7,256]{2,1,0:T(8,128)S(1)}, s32[256]{0:T(256)S(1)}, ...), branch_computations={%region_6.8_spmd, %region_7.11_spmd} | conditional | flops 242756096 | bytes 11890720 | solution.py:113
  126.0 1.1 fusion.5
  131.8 3.2 %conditional.3 = ((f32[256,7]{0,1:T(8,128)S(1)}, f32[256,7]{0,1:T(8,128)S(1)}, f32[256,7,128]{2,0,1:T(8,128)S(1)})) conditional(s32[]{:T(128)} %convert_element_type.37, (f32[256,7]{0,1:T(8,128)S(1)}, f32[256,7]{0,1:T(8,128)S(1)}, f32[256,7,128]{2,0,1:T(8,128)S(1)}) %tuple.80, (f32[4,7,256]{2,1,0:T(8,128)S(1)}, s32[256]{0:T(256)S(1)}, ...), branch_computations={%region_6.8_spmd, %region_7.11_spmd} | conditional | flops 242756096 | bytes 11890720 | solution.py:113
  133.8 1.1 fusion.5
  135.8 19.3 %all_to_all.61 = bf16[256,1,7,128]{3,2,1,0:T(8,128)(2,1)S(1)} all-to-all(bf16[256,1,7,128]{3,2,1,0:T(8,128)(2,1)S(1)} %fusion.24), channel_id=1, replica_groups=mesh['head'=4,'ctx'=8] {'head'}, dimensions={0} | all-to-all | bytes 917504 | tf_op jit(solution)/shard_map/all_to_all | solution.py:127
  155.2 1.3 reshape_reshape.3
  (234 shorter events, 52.7 us)
Async XLA Ops:
  6.5 21.3 %copy-start = (bf16[64,3584]{1,0:T(8,128)(2,1)S(1)}, bf16[64,3584]{1,0:T(8,128)(2,1)}, u32[]{:S(2)}) copy-start(bf16[64,3584]{1,0:T(8,128)(2,1)} %param.14) | copy-start | bytes 1376260
  6.5 21.1 %copy-start.3 = (s32[28]{0:T(128)S(1)}, s32[28]{0:T(128)}, u32[]{:S(2)}) copy-start(s32[28]{0:T(128)} %param.19) | copy-start | bytes 340
  6.5 41.2 %all-gather.3.cloned.1.call-start = ((), (), s32[]{:S(2)}) async-start(), calls=%async_computation.4 | async-start | bytes 1179648 | tf_op jit(solution)/shard_map/all_gather | solution.py:97
  24.2 9.2 %all-to-all-start.1 = ((bf16[64,4,2,128]{3,0,2,1:T(8,128)(2,1)}), bf16[64,4,2,128]{3,0,2,1:T(8,128)(2,1)S(1)}, u32[]{:S(2)}, u32[]{:S(2)}) async-start(bf16[64,4,2,128]{3,0,2,1:T(8,128)(2,1)} %bitcast.13), calls=%async_computation.1 | async-start | bytes 262144 | tf_op jit(solution)/shard_map/all_to_all | solution.py:73
  27.9 9.8 %copy-start.1 = (s32[16,28]{1,0:T(8,128)S(1)}, s32[16,28]{1,0:T(8,128)}, u32[]{:S(2)}) copy-start(s32[16,28]{1,0:T(8,128)} %param.18) | copy-start | bytes 5380
  28.0 10.5 %copy-start.2 = (s32[16,28,16]{1,2,0:T(8,128)S(1)}, s32[16,28,16]{1,2,0:T(8,128)}, u32[]{:S(2)}) copy-start(s32[16,28,16]{1,2,0:T(8,128)} %param.17) | copy-start | bytes 86020
  33.5 14.2 %all-to-all-start.2 = ((bf16[64,4,7,128]{3,0,2,1:T(8,128)(2,1)}), bf16[64,4,7,128]{3,0,2,1:T(8,128)(2,1)S(1)}, u32[]{:S(2)}, u32[]{:S(2)}) async-start(bf16[64,4,7,128]{3,0,2,1:T(8,128)(2,1)} %broadcast_select_fusion), calls=%async_computation.2 | async-start | bytes 917504 | tf_op jit(solution)/shard_map/all_to_all | solution.py:71
  36.9 35.5 %all-gather.5.cloned.1.call-start = ((), (), s32[]{:S(2)}) async-start(), calls=%async_computation.5 | async-start | bytes 1179648 | tf_op jit(solution)/shard_map/all_gather | solution.py:98
Sparse Core Ops, SparseCore 0:
  24.4 22.5 all-gather.2
  48.9 23.4 all-gather.4
where the time goes:
time: 164 us; the launch traced here: 163 us
  waiting for transfers between devices  34 us (21%)
  local copies, waits for them, and re-layouts  33.7 us (21%)
  blocking collectives  31.5 us (19%)
  other arithmetic  22.6 us (14%)
  matrix products  14.3 us (9%)
  between operations  13.6 us (8%)
  starting transfers between devices  6.84 us (4%)
  loops' own time  6.67 us (4%)
    all_gather x1, waiting for transfers between devices, local(): value_piece = lax.all_gather(value_rows, 'ctx', axis=0, tiled=True)  24.7 us
    all_to_all x1, blocking collectives, local(): lax.all_to_all(attended, 'head', split_axis=0, concat_axis=1, tiled=True)  19.3 us
    all_to_all x1, blocking collectives, local(): lax.all_to_all(key_sent, 'head', split_axis=1, concat_axis=0, tiled=True)  12.2 us
    dot_general x8, matrix products, update_lanes(): jnp.einsum('qgk,kgd->qgd', weights.astype(jnp.bfloat16), value_lanes, pre...  9.06 us
    reduce_or x8, other arithmetic, one_shard(): jnp.any(allowed)  8.85 us
    dynamic_slice x8, local copies, waits for them, and re-layouts, one_shard(): lax.dynamic_slice_in_dim(value_piece, number * row_count, row_count, 0)  8 us
    another operation x1, loops' own time, local(): folded = lax.fori_loop(0, shard_total, one_shard, initial)  5.91 us
    all_to_all x1, waiting for transfers between devices, local(): lax.all_to_all(query_sent, 'head', split_axis=1, concat_axis=0, tiled=True)  5.34 us
  transfers between devices with their start and end apart: 4, of which 3 were waited for; matrix products, arithmetic and copies ran while one was open for 4% of the time, Pallas kernels for 0%

commit v1 on v0

--- a/solution.py
+++ b/solution.py
@@ -4,6 +4,8 @@
 import jax
 import jax.numpy as jnp
 from jax import lax
+from jax.experimental import pallas as pl
+from jax.experimental.pallas import tpu as pltpu
 from jax.sharding import PartitionSpec as P
 
 H = 28
@@ -13,6 +15,7 @@
 
 
 FLOOR = -1e30
+MESH = pl.DeviceIdType.MESH
 
 
 def positions(stripes, stripe_len, device, ctx_total):
@@ -130,9 +133,260 @@
     return returned.reshape(local_tokens, H * HD)
 
 
+LOG2E = 1.4426950408889634
+MASKED = -1e30
+
+
+def plane_kernel(
+    q_ref, k_ref, v_ref, table_ref, order_ref, out_ref,
+    k_all, v_all, q_in, q_ext, acc, top, total, done, entries,
+    local_sems, send_sems, recv_sems,
+):
+    z = lax.axis_index("head")
+    ctx = lax.axis_index("ctx")
+    planes = lax.axis_size("head")
+    tokens = q_ref.shape[0]
+    per_group = H // KVH
+    rows = per_group * tokens
+    core = ctx % 2
+    x_pos = (ctx // 2) % 2
+    y_pos = ctx // 4
+    sib = ctx + 1 - 2 * core
+    xn = ctx + 2 - 4 * x_pos
+    yn = ctx + 4 - 8 * y_pos
+    dg = xn + 4 - 8 * y_pos
+    to_sib = 1 - 2 * core
+    query_block = (z * 8 + ctx) * tokens // BLOCK
+    bufs = (k_all, v_all)
+    heres = (k_ref, v_ref)
+
+    local_copies = [
+        pltpu.make_async_copy(q_ref, q_in, local_sems.at[0]),
+        pltpu.make_async_copy(table_ref.at[query_block], entries, local_sems.at[1]),
+        pltpu.make_async_copy(k_ref, k_all.at[z * 8 + ctx], local_sems.at[2]),
+        pltpu.make_async_copy(v_ref, v_all.at[z * 8 + ctx], local_sems.at[3]),
+    ]
+    for copy in local_copies:
+        copy.start()
+
+    barrier = pltpu.get_barrier_semaphore()
+    for near in (sib, xn, yn):
+        pl.semaphore_signal(
+            barrier, inc=1, device_id={"head": z, "ctx": near}, device_id_type=MESH
+        )
+
+    @pl.when(z > 0)
+    def _():
+        pl.semaphore_signal(
+            barrier, inc=1, device_id={"head": z - 1, "ctx": ctx}, device_id_type=MESH
+        )
+
+    @pl.when(z < planes - 1)
+    def _():
+        pl.semaphore_signal(
+            barrier, inc=1, device_id={"head": z + 1, "ctx": ctx}, device_id_type=MESH
+        )
+
+    pl.semaphore_wait(
+        barrier, 3 + (z > 0).astype(jnp.int32) + (z < planes - 1).astype(jnp.int32)
+    )
+
+    def push(which, k, slot, kind, head_to, ctx_to, own=False):
+        place = bufs[which].at[(z - k) * 8 + slot]
+        return pltpu.make_async_remote_copy(
+            src_ref=heres[which] if own else place,
+            dst_ref=place,
+            send_sem=send_sems.at[k, kind],
+            recv_sem=recv_sems.at[z - k, slot, which],
+            device_id={"head": head_to, "ctx": ctx_to},
+            device_id_type=MESH,
+        )
+
+    def arrived(which, k, slot):
+        push(which, k, slot, 0, z, sib).wait_recv()
+
+    def column(k):
+        @pl.when(z >= k)
+        def _():
+            for which in (0, 1):
+                if k > 0:
+                    arrived(which, k, ctx)
+
+                @pl.when(z < planes - 1)
+                def _():
+                    push(which, k, ctx, which, z + 1, ctx, k == 0).start()
+
+                push(which, k, ctx, 2 + which, z, xn, k == 0).start()
+                push(which, k, ctx, 4 + which, z, yn, k == 0).start()
+                push(which, k, ctx, 8 + which, z, sib, k == 0).start()
+
+    def across(k):
+        @pl.when(z >= k)
+        def _():
+            arrived(0, k, xn)
+            push(0, k, xn, 6, z, yn).start()
+            push(0, k, xn, 10, z, sib).start()
+            arrived(1, k, yn)
+            push(1, k, yn, 7, z, xn).start()
+            push(1, k, yn, 13, z, sib).start()
+            arrived(0, k, yn)
+            push(0, k, yn, 12, z, sib).start()
+            arrived(1, k, xn)
+            push(1, k, xn, 11, z, sib).start()
+
+    def corner(k):
+        @pl.when(z >= k)
+        def _():
+            for which in (0, 1):
+                arrived(which, k, dg)
+                push(which, k, dg, 14 + which, z, sib).start()
+
+    def beside(k):
+        @pl.when(z >= k)
+        def _():
+            for slot in (ctx, xn, yn, dg):
+                for which in (0, 1):
+                    arrived(which, k, slot + to_sib)
+
+    def sent(k):
+        @pl.when(z >= k)
+        def _():
+            for which in (0, 1):
+                @pl.when(z < planes - 1)
+                def _():
+                    push(which, k, ctx, which, z + 1, ctx).wait_send()
+            for kind in range(2, 16):
+                push(0, k, ctx, kind, z, sib).wait_send()
+
+    def prepare():
+        for copy in local_copies:
+            copy.wait()
+        listed = entries[...]
+        width = listed.shape[1]
+        spot = lax.broadcasted_iota(jnp.int32, listed.shape, 1)
+        last = jnp.min(jnp.where(listed == query_block, spot, width), axis=1, keepdims=True)
+        listed = jnp.where(spot <= last, listed, -1)
+        lane = lax.broadcasted_iota(jnp.int32, (H, HD), 1)
+        bias = jnp.full((H, HD), MASKED, jnp.float32)
+        for e in range(width):
+            bias = jnp.where(listed[:, e:e + 1] == lane, 0.0, bias)
+        for h in range(H):
+            group, row = h // per_group, (h % per_group) * tokens
+            q_ext[group, row:row + tokens, :HD] = q_in[:, h * HD:(h + 1) * HD]
+            q_ext[group, row:row + tokens, HD:] = jnp.broadcast_to(
+                bias[h:h + 1, :], (tokens, HD)
+            ).astype(jnp.bfloat16)
+
+    def attend(k):
+        @pl.when(z >= k)
+        def _():
+            plane = z - k
+            keys_here = 8 * tokens
+            factor = LOG2E / math.sqrt(HD)
+            key_row = lax.broadcasted_iota(jnp.int32, (keys_here, HD), 0)
+            key_lane = lax.broadcasted_iota(jnp.int32, (keys_here, HD), 1)
+            block_of = (plane * keys_here + key_row) // BLOCK
+            onehot = jnp.where(block_of == key_lane, 1.0, 0.0).astype(jnp.bfloat16)
+
+            def one_group(j, carry):
+                cols = pl.ds(pl.multiple_of(j * HD, HD), HD)
+                key = k_all[pl.ds(plane * 8, 8), :, cols].reshape(keys_here, HD)
+                value = v_all[pl.ds(plane * 8, 8), :, cols].reshape(keys_here, HD)
+                key = jnp.concatenate([key, onehot], axis=1)
+                s = lax.dot_general(
+                    q_ext[j], key, (((1,), (1,)), ((), ())), preferred_element_type=jnp.float32
+                )
+                if k == 0:
+                    row_pos = ctx * tokens + lax.broadcasted_iota(jnp.int32, s.shape, 0) % tokens
+                    col_pos = lax.broadcasted_iota(jnp.int32, s.shape, 1)
+                    s = jnp.where(col_pos <= row_pos, s, MASKED)
+                high = jnp.max(s, axis=1, keepdims=True)
+                if k > 0:
+                    old = top[j][:, :1]
+                    high = jnp.maximum(high, old)
+                    shrink = jnp.exp2((old - high) * factor)
+                w = jnp.exp2((s - high) * factor)
+                part = w[:, :HD]
+                for cut in range(1, keys_here // HD):
+                    part = part + w[:, cut * HD:(cut + 1) * HD]
+                mixed = jnp.dot(
+                    w.astype(jnp.bfloat16), value, preferred_element_type=jnp.float32
+                )
+                if k > 0:
+                    part = part + total[j] * shrink
+                    mixed = mixed + acc[j] * shrink
+                top[j] = jnp.broadcast_to(high, (rows, HD))
+                total[j] = part
+                acc[j] = mixed
+                return carry
+
+            lax.fori_loop(0, KVH, one_group, 0)
+
+    column(0)
+    prepare()
+    across(0)
+    column(1)
+    corner(0)
+    for k in range(4):
+        if k < 3:
+            across(k + 1)
+        beside(k)
+        if k == 3:
+            pass
+        attend(k)
+        if k < 2:
+            column(k + 2)
+        if k < 3:
+            corner(k + 1)
+
+    def finish(j, carry):
+        summed = jnp.sum(total[j], axis=1, keepdims=True)
+        done[pl.ds(j * per_group, per_group)] = (
+            (acc[j] / summed).astype(jnp.bfloat16).reshape(per_group, tokens, HD)
+        )
+        return carry
+
+    lax.fori_loop(0, KVH, finish, 0)
+    for place in range(H):
+        out_ref[:, place * HD:(place + 1) * HD] = done[order_ref[place]]
+    for k in range(4):
+        sent(k)
+
+
+def planes_local(queries, keys, values, block_index, block_count, head_order):
+    tokens = queries.shape[0]
+    planes = lax.axis_size("head")
+    rows = H // KVH * tokens
+    any_spec = pl.BlockSpec(memory_space=pl.ANY)
+    return pl.pallas_call(
+        plane_kernel,
+        out_shape=jax.ShapeDtypeStruct(queries.shape, jnp.bfloat16),
+        in_specs=[any_spec] * 4 + [pl.BlockSpec(memory_space=pltpu.SMEM)],
+        out_specs=pl.BlockSpec(memory_space=pltpu.VMEM),
+        scratch_shapes=[
+            pltpu.VMEM((planes * 8, tokens, KVH * HD), jnp.bfloat16),
+            pltpu.VMEM((planes * 8, tokens, KVH * HD), jnp.bfloat16),
+            pltpu.VMEM(queries.shape, jnp.bfloat16),
+            pltpu.VMEM((KVH, rows, 2 * HD), jnp.bfloat16),
+            pltpu.VMEM((KVH, rows, HD), jnp.float32),
+            pltpu.VMEM((KVH, rows, HD), jnp.float32),
+            pltpu.VMEM((KVH, rows, HD), jnp.float32),
+            pltpu.VMEM((H, tokens, HD), jnp.bfloat16),
+            pltpu.VMEM(block_index.shape[1:], jnp.int32),
+            pltpu.SemaphoreType.DMA((4,)),
+            pltpu.SemaphoreType.DMA((planes, 16)),
+            pltpu.SemaphoreType.DMA((planes, 8, 2)),
+        ],
+        compiler_params=pltpu.CompilerParams(
+            collective_id=0, has_side_effects=True, vmem_limit_bytes=48 * 1024 * 1024
+        ),
+    )(queries, keys, values, block_index, head_order)
+
+
 def solution(mesh):
+    in_planes = mesh.shape["head"] == 4 and mesh.shape["ctx"] == 8
     return jax.shard_map(
-        local,
+        planes_local if in_planes else local,
         mesh=mesh,
         in_specs=(
             P(("head", "ctx"), None),

time: 164 us -> 46.7 us (0.28)
  the two profiles are of different devices: /device:TPU:0 before, /device:TPU:25 now
where the time goes in v1:
time: 46.7 us; the launch traced here: 46.6 us
  Pallas kernels  43.6 us (93%)
  local copies, waits for them, and re-layouts  2.9 us (6%)
    pallas_call x1, Pallas kernels, planes_local(): pl.pallas_call(plane_kernel, out_shape=jax.ShapeDtypeStruct(queries.shape...  43.6 us
    unnamed x10, local copies, waits for them, and re-layouts  2.9 us

profile of v1, /device:TPU:25, one launch (start us, length us, event | category | flops | bytes accessed | tf_op | source)
XLA Modules:
  0.0 46.6 jit_solution(14564111790043225579)
XLA Ops:
  0.0 0.0 copy-start.3
  0.0 0.0 copy-start.2
  0.0 0.0 copy-start.1
  0.0 1.1 %copy.6.table_ref = s32[16,28,16]{2,1,0:T(8,128)S(1)} copy(s32[16,28,16]{1,2,0:T(8,128)} %param.9) | data formatting | bytes 57344 | tf_op args[3]
  1.1 0.0 copy-done.3
  1.1 0.0 copy-done.2
  1.1 0.0 copy-done.1
  1.1 0.0 copy-start
  1.2 1.0 %copy-done = bf16[64,3584]{1,0:T(8,128)(2,1)S(1)} copy-done((bf16[64,3584]{1,0:T(8,128)(2,1)S(1)}, bf16[64,3584]{1,0:T(8,128)(2,1)}, u32[]{:S(2)}) %copy-start) | copy-done | bytes 458776
  2.2 43.6 %shard_map.55 = bf16[64,3584]{1,0:T(8,128)(2,1)S(1)} custom-call(bf16[64,3584]{1,0:T(8,128)(2,1)S(1)} %copy-done, bf16[64,512]{1,0:T(8,128)(2,1)S(1)} %copy-done.1, bf16[64,512]{1,0:T(8,128)(2,1)S(1)} %copy-done.2, s32[16,28,16]{2,1,0:T(8,128)S(1)} %copy.6.table_ref, s32[28]{0:T(128)S(1)} %copy-done.3), custom_call_target="tpu_custom_call" | custom-call | tf_op jit(solution)/shard_map/pallas_call | solution.py:361
  45.8 0.8 %copy.8 = bf16[64,3584]{1,0:T(8,128)(2,1)} copy(bf16[64,3584]{1,0:T(8,128)(2,1)S(1)} %shard_map.55) | data formatting | bytes 917504
Async XLA Ops:
  0.0 1.1 %copy-start.3 = (s32[28]{0:T(128)S(1)}, s32[28]{0:T(128)}, u32[]{:S(2)}) copy-start(s32[28]{0:T(128)} %order_ref.1) | copy-start | bytes 340
  0.0 1.1 %copy-start.2 = (bf16[64,512]{1,0:T(8,128)(2,1)S(1)}, bf16[64,512]{1,0:T(8,128)(2,1)}, u32[]{:S(2)}) copy-start(bf16[64,512]{1,0:T(8,128)(2,1)} %v_ref.1) | copy-start | bytes 196612
  0.0 1.1 %copy-start.1 = (bf16[64,512]{1,0:T(8,128)(2,1)S(1)}, bf16[64,512]{1,0:T(8,128)(2,1)}, u32[]{:S(2)}) copy-start(bf16[64,512]{1,0:T(8,128)(2,1)} %k_ref.1) | copy-start | bytes 196612
  1.1 1.0 %copy-start = (bf16[64,3584]{1,0:T(8,128)(2,1)S(1)}, bf16[64,3584]{1,0:T(8,128)(2,1)}, u32[]{:S(2)}) copy-start(bf16[64,3584]{1,0:T(8,128)(2,1)} %q_ref.1) | copy-start | bytes 1376260

commit v2 on v0

--- a/solution.py
+++ b/solution.py
@@ -4,6 +4,8 @@
 import jax
 import jax.numpy as jnp
 from jax import lax
+from jax.experimental import pallas as pl
+from jax.experimental.pallas import tpu as pltpu
 from jax.sharding import PartitionSpec as P
 
 H = 28
@@ -13,6 +15,7 @@
 
 
 FLOOR = -1e30
+MESH = pl.DeviceIdType.MESH
 
 
 def positions(stripes, stripe_len, device, ctx_total):
@@ -130,9 +133,357 @@
     return returned.reshape(local_tokens, H * HD)
 
 
+LOG2E = 1.4426950408889634
+MASKED = -1e30
+
+
+def plane_kernel(
+    q_ref, k_ref, v_ref, table_ref, order_ref, out_ref,
+    k_all, v_all, q_in, q_ext, acc, top, total, lists, bias_by_block, bias_by_head,
+    done, leaving, local_sems, swap_send, swap_recv, send_sems, recv_sems,
+):
+    z = lax.axis_index("head")
+    ctx = lax.axis_index("ctx")
+    planes = lax.axis_size("head")
+    tokens = q_ref.shape[0]
+    per_group = H // KVH
+    groups = KVH // 2
+    heads = H // 2
+    both = 2 * tokens
+    rows = per_group * both
+    half = groups * HD
+    core = ctx % 2
+    other = 1 - core
+    chip = ctx // 2
+    x_chip = chip + 1 - 2 * (chip % 2)
+    y_chip = chip + 2 - 4 * (chip // 2)
+    d_chip = x_chip + y_chip - chip
+    sib = 2 * chip + other
+    query_block = (z * 4 + chip) * both // BLOCK
+    bufs = (k_all, v_all)
+    heres = (k_ref, v_ref)
+
+    def columns(which_core, width):
+        return pl.ds(pl.multiple_of(which_core * width, width), width)
+
+    def token_rows(which_core):
+        return pl.ds(pl.multiple_of(which_core * tokens, tokens), tokens)
+
+    local_copies = [
+        pltpu.make_async_copy(
+            q_ref.at[:, columns(core, heads * HD)], q_in.at[core], local_sems.at[0]
+        ),
+        pltpu.make_async_copy(table_ref.at[query_block], lists, local_sems.at[1]),
+    ]
+    for which in (0, 1):
+        local_copies.append(pltpu.make_async_copy(
+            heres[which].at[:, columns(core, half)],
+            bufs[which].at[z * 4 + chip, token_rows(core)],
+            local_sems.at[2 + which],
+        ))
+    for copy in local_copies:
+        copy.start()
+
+    barrier = pltpu.get_barrier_semaphore()
+
+    def greet(head_to, ctx_to):
+        pl.semaphore_signal(
+            barrier, inc=1, device_id={"head": head_to, "ctx": ctx_to}, device_id_type=MESH
+        )
+
+    greet(z, sib)
+    for which_core in (core, other):
+        greet(z, 2 * x_chip + which_core)
+        greet(z, 2 * y_chip + which_core)
+
+    @pl.when(z > 0)
+    def _():
+        greet(z - 1, ctx)
+        greet(z - 1, sib)
+
+    @pl.when(z < planes - 1)
+    def _():
+        greet(z + 1, ctx)
+        greet(z + 1, sib)
+
+    pl.semaphore_wait(
+        barrier, 5 + 2 * (z > 0).astype(jnp.int32) + 2 * (z < planes - 1).astype(jnp.int32)
+    )
+
+    def piece(which, to_core, kind, head_to, ctx_to):
+        return pltpu.make_async_remote_copy(
+            src_ref=heres[which].at[:, columns(to_core, half)],
+            dst_ref=bufs[which].at[z * 4 + chip, token_rows(core)],
+            send_sem=send_sems.at[0, kind],
+            recv_sem=recv_sems.at[z, chip, which, core],
+            device_id={"head": head_to, "ctx": ctx_to},
+            device_id_type=MESH,
+        )
+
+    def whole(which, k, slot, kind, head_to, ctx_to):
+        place = bufs[which].at[(z - k) * 4 + slot]
+        return pltpu.make_async_remote_copy(
+            src_ref=place,
+            dst_ref=place,
+            send_sem=send_sems.at[k, kind],
+            recv_sem=recv_sems.at[z - k, slot, which, 0],
+            device_id={"head": head_to, "ctx": ctx_to},
+            device_id_type=MESH,
+        )
+
+    def piece_arrived(which, plane, slot, from_core):
+        place = bufs[which].at[plane * 4 + slot, token_rows(from_core)]
+        pltpu.make_async_remote_copy(
+            src_ref=place,
+            dst_ref=place,
+            send_sem=send_sems.at[0, 0],
+            recv_sem=recv_sems.at[plane, slot, which, from_core],
+            device_id={"head": z, "ctx": sib},
+            device_id_type=MESH,
+        ).wait_recv()
+
+    def whole_arrived(which, k, slot):
+        whole(which, k, slot, 0, z, sib).wait_recv()
+
+    def swap(src, dst, number):
+        return pltpu.make_async_remote_copy(
+            src_ref=src,
+            dst_ref=dst,
+            send_sem=swap_send.at[number],
+            recv_sem=swap_recv.at[number],
+            device_id={"head": z, "ctx": sib},
+            device_id_type=MESH,
+        )
+
+    q_swap = swap(q_ref.at[:, columns(other, heads * HD)], q_in.at[core], 0)
+    q_got = swap(q_in.at[other], q_in.at[other], 0)
+
+    def own_pieces():
+        for which in (0, 1):
+            for cross, to_core in enumerate((core, other)):
+                number = 2 * which + cross
+
+                @pl.when(z < planes - 1)
+                def _():
+                    piece(which, to_core, number, z + 1, 2 * chip + to_core).start()
+
+                piece(which, to_core, 4 + number, z, 2 * x_chip + to_core).start()
+                piece(which, to_core, 8 + number, z, 2 * y_chip + to_core).start()
+            piece(which, other, 12 + which, z, sib).start()
+
+    def column(k):
+        @pl.when(z >= k)
+        def _():
+            for which in (0, 1):
+                if k == 1:
+                    piece_arrived(which, z - 1, chip, core)
+                    piece_arrived(which, z - 1, chip, other)
+                else:
+                    whole_arrived(which, k, chip)
+
+                @pl.when(z < planes - 1)
+                def _():
+                    whole(which, k, chip, which, z + 1, ctx).start()
+
+                whole(which, k, chip, 2 + which, z, 2 * x_chip + core).start()
+                whole(which, k, chip, 4 + which, z, 2 * y_chip + core).start()
+
+    def side_arrived(which, k, slot):
+        if k == 0:
+            piece_arrived(which, z, slot, core)
+            piece_arrived(which, z, slot, other)
+        else:
+            whole_arrived(which, k, slot)
+
+    def across(k):
+        @pl.when(z >= k)
+        def _():
+            side_arrived(0, k, x_chip)
+            whole(0, k, x_chip, 14, z, 2 * y_chip + core).start()
+            side_arrived(1, k, y_chip)
+            whole(1, k, y_chip, 15, z, 2 * x_chip + core).start()
+
+    def rest(k):
+        @pl.when(z >= k)
+        def _():
+            side_arrived(1, k, x_chip)
+            side_arrived(0, k, y_chip)
+            if k == 0:
+                for which in (0, 1):
+                    piece_arrived(which, z, chip, other)
+            for which in (0, 1):
+                whole_arrived(which, k, d_chip)
+
+    def sent(k):
+        @pl.when(z >= k)
+        def _():
+            if k == 0:
+                @pl.when(z < planes - 1)
+                def _():
+                    for kind in range(4):
+                        piece(0, core, kind, z, sib).wait_send()
+
+                for kind in range(4, 14):
+                    piece(0, core, kind, z, sib).wait_send()
+            else:
+                @pl.when(z < planes - 1)
+                def _():
+                    for kind in range(2):
+                        whole(0, k, chip, kind, z, sib).wait_send()
+
+                for kind in range(2, 6):
+                    whole(0, k, chip, kind, z, sib).wait_send()
+            for kind in (14, 15):
+                whole(0, k, chip, kind, z, sib).wait_send()
+
+    def prepare():
+        for copy in local_copies:
+            copy.wait()
+        listed = lists[...]
+        width = listed.shape[0]
+        spot = lax.broadcasted_iota(jnp.int32, listed.shape, 0)
+        last = jnp.min(jnp.where(listed == query_block, spot, width), axis=0, keepdims=True)
+        listed = jnp.where(spot <= last, listed, -1)
+        block = lax.broadcasted_iota(jnp.int32, (HD, H), 0)
+        bias = jnp.full((HD, H), MASKED, jnp.float32)
+        for e in range(width):
+            bias = jnp.where(listed[e:e + 1, :] == block, 0.0, bias)
+        bias_by_block[...] = jnp.zeros_like(bias_by_block)
+        bias_by_block[:, :H] = bias
+        bias_by_head[...] = bias_by_block[...].T
+        q_got.wait_recv()
+        for h in range(heads):
+            group, row = h // per_group, (h % per_group) * both
+            for part in (0, 1):
+                start = row + part * tokens
+                q_ext[group, start:start + tokens, :HD] = q_in[part, :, h * HD:(h + 1) * HD]
+            q_ext[group, row:row + both, HD:] = jnp.broadcast_to(
+                bias_by_head[pl.ds(core * heads + h, 1), :], (both, HD)
+            ).astype(jnp.bfloat16)
+
+    keys_here = 4 * both
+    cuts = [slice(i * HD, (i + 1) * HD) for i in range(keys_here // HD)]
+    factor = LOG2E / math.sqrt(HD)
+
+    def attend(k, group):
+        @pl.when(z >= k)
+        def _():
+            plane = z - k
+            key_row = lax.broadcasted_iota(jnp.int32, (keys_here, HD), 0)
+            key_lane = lax.broadcasted_iota(jnp.int32, (keys_here, HD), 1)
+            block_of = (plane * keys_here + key_row) // BLOCK
+            onehot = jnp.where(block_of == key_lane, 1.0, 0.0).astype(jnp.bfloat16)
+            cols = slice(group * HD, (group + 1) * HD)
+            key = k_all[pl.ds(plane * 4, 4), :, cols].reshape(keys_here, HD)
+            value = v_all[pl.ds(plane * 4, 4), :, cols].reshape(keys_here, HD)
+            s = lax.dot_general(
+                q_ext[group],
+                jnp.concatenate([key, onehot], axis=1),
+                (((1,), (1,)), ((), ())),
+                preferred_element_type=jnp.float32,
+            )
+            if k == 0:
+                row_pos = chip * both + lax.broadcasted_iota(jnp.int32, s.shape, 0) % both
+                col_pos = lax.broadcasted_iota(jnp.int32, s.shape, 1)
+                s = jnp.where(col_pos <= row_pos, s, MASKED)
+            high = s[:, cuts[0]]
+            for cut in cuts[1:]:
+                high = jnp.maximum(high, s[:, cut])
+            high = jnp.broadcast_to(jnp.max(high, axis=1, keepdims=True), (rows, HD))
+            if k > 0:
+                old = top[group]
+                high = jnp.maximum(high, old)
+                shrink = jnp.exp2((old - high) * factor)
+            parts = [jnp.exp2((s[:, cut] - high) * factor) for cut in cuts]
+            w = jnp.concatenate([part.astype(jnp.bfloat16) for part in parts], axis=1)
+            part = parts[0]
+            for more in parts[1:]:
+                part = part + more
+            mixed = jnp.dot(w, value, preferred_element_type=jnp.float32)
+            if k > 0:
+                part = part + total[group] * shrink
+                mixed = mixed + acc[group] * shrink
+            top[group] = high
+            total[group] = part
+            acc[group] = mixed
+
+    own_pieces()
+    q_swap.start()
+    prepare()
+    across(0)
+    column(1)
+    rest(0)
+    for k in range(4):
+        attend(k, 0)
+        if k < 3:
+            across(k + 1)
+        if k < 2:
+            column(k + 2)
+        attend(k, 1)
+        if k < 3:
+            rest(k + 1)
+
+    mine = pl.ds(core * heads, heads)
+    home = swap(leaving, done.at[mine], 1)
+    for group in range(groups):
+        summed = jnp.sum(total[group], axis=1, keepdims=True)
+        result = (acc[group] / summed).astype(jnp.bfloat16)
+        result = result.reshape(per_group, 2, tokens, HD)
+        here = jnp.where(core == 0, result[:, 0], result[:, 1])
+        there = jnp.where(core == 0, result[:, 1], result[:, 0])
+        done[pl.ds(core * heads + group * per_group, per_group)] = here
+        leaving[group * per_group:(group + 1) * per_group] = there
+    home.start()
+    for k in range(4):
+        sent(k)
+    q_swap.wait_send()
+    swap(leaving, done.at[pl.ds(other * heads, heads)], 1).wait_recv()
+    for place in range(H):
+        out_ref[:, place * HD:(place + 1) * HD] = done[order_ref[place]]
+    home.wait_send()
+
+
+def planes_local(queries, keys, values, block_index, block_count, head_order):
+    tokens = queries.shape[0]
+    planes = lax.axis_size("head")
+    rows = H // KVH * 2 * tokens
+    groups = KVH // 2
+    table = block_index.transpose(0, 2, 1)
+    any_spec = pl.BlockSpec(memory_space=pl.ANY)
+    return pl.pallas_call(
+        plane_kernel,
+        out_shape=jax.ShapeDtypeStruct(queries.shape, jnp.bfloat16),
+        in_specs=[any_spec] * 4 + [pl.BlockSpec(memory_space=pltpu.SMEM)],
+        out_specs=pl.BlockSpec(memory_space=pltpu.VMEM),
+        scratch_shapes=[
+            pltpu.VMEM((planes * 4, 2 * tokens, groups * HD), jnp.bfloat16),
+            pltpu.VMEM((planes * 4, 2 * tokens, groups * HD), jnp.bfloat16),
+            pltpu.VMEM((2, tokens, H // 2 * HD), jnp.bfloat16),
+            pltpu.VMEM((groups, rows, 2 * HD), jnp.bfloat16),
+            pltpu.VMEM((groups, rows, HD), jnp.float32),
+            pltpu.VMEM((groups, rows, HD), jnp.float32),
+            pltpu.VMEM((groups, rows, HD), jnp.float32),
+            pltpu.VMEM(table.shape[1:], jnp.int32),
+            pltpu.VMEM((HD, HD), jnp.float32),
+            pltpu.VMEM((HD, HD), jnp.float32),
+            pltpu.VMEM((H, tokens, HD), jnp.bfloat16),
+            pltpu.VMEM((H // 2, tokens, HD), jnp.bfloat16),
+            pltpu.SemaphoreType.DMA((4,)),
+            pltpu.SemaphoreType.DMA((2,)),
+            pltpu.SemaphoreType.DMA((2,)),
+            pltpu.SemaphoreType.DMA((planes, 16)),
+            pltpu.SemaphoreType.DMA((planes, 4, 2, 2)),
+        ],
+        compiler_params=pltpu.CompilerParams(
+            collective_id=0, has_side_effects=True, vmem_limit_bytes=60 * 1024 * 1024
+        ),
+    )(queries, keys, values, table, head_order)
+
+
 def solution(mesh):
+    in_planes = mesh.shape["head"] == 4 and mesh.shape["ctx"] == 8
     return jax.shard_map(
-        local,
+        planes_local if in_planes else local,
         mesh=mesh,
         in_specs=(
             P(("head", "ctx"), None),

time: 164 us -> 35.1 us (0.21)
  the two profiles are of different devices: /device:TPU:0 before, /device:TPU:25 now
where the time goes in v2:
time: 35.1 us; the launch traced here: 34.9 us
  Pallas kernels  33.1 us (94%)
  local copies, waits for them, and re-layouts  1.82 us (5%)
    pallas_call x1, Pallas kernels, planes_local(): pl.pallas_call(plane_kernel, out_shape=jax.ShapeDtypeStruct(queries.shape...  33.1 us
    unnamed x1, local copies, waits for them, and re-layouts  1.82 us

profile of v2, /device:TPU:25, one launch (start us, length us, event | category | flops | bytes accessed | tf_op | source)
XLA Modules:
  0.0 34.9 jit_solution(17056070905292493979)
XLA Ops:
  0.0 33.1 %shard_map.55 = bf16[64,3584]{1,0:T(8,128)(2,1)} custom-call(bf16[64,3584]{1,0:T(8,128)(2,1)} %q_ref.1, bf16[64,512]{1,0:T(8,128)(2,1)} %k_ref.1, bf16[64,512]{1,0:T(8,128)(2,1)} %v_ref.1, s32[16,16,28]{2,1,0:T(8,128)} %bitcast.1, s32[28]{0:T(128)} %order_ref.1), custom_call_target="tpu_custom_call" | custom-call | tf_op jit(solution)/shard_map/pallas_call | solution.py:453
  33.1 1.8 %copy.7 = bf16[64,3584]{1,0:T(8,128)(2,1)} copy(bf16[64,3584]{1,0:T(8,128)(2,1)} %shard_map.55) | data formatting | bytes 917504

commit v3 on v2

--- a/solution.py
+++ b/solution.py
@@ -133,13 +133,12 @@
     return returned.reshape(local_tokens, H * HD)
 
 
-LOG2E = 1.4426950408889634
 MASKED = -1e30
 
 
 def plane_kernel(
     q_ref, k_ref, v_ref, table_ref, order_ref, out_ref,
-    k_all, v_all, q_in, q_ext, acc, top, total, lists, bias_by_block, bias_by_head,
+    k_all, v_all, q_in, q_rows, q_ext, acc, top, total, lists, bias_by_block, bias_by_head,
     done, leaving, local_sems, swap_send, swap_recv, send_sems, recv_sems,
 ):
     z = lax.axis_index("head")
@@ -356,14 +355,16 @@
             group, row = h // per_group, (h % per_group) * both
             for part in (0, 1):
                 start = row + part * tokens
-                q_ext[group, start:start + tokens, :HD] = q_in[part, :, h * HD:(h + 1) * HD]
-            q_ext[group, row:row + both, HD:] = jnp.broadcast_to(
+                q_rows[group, start:start + tokens, :HD] = q_in[part, :, h * HD:(h + 1) * HD]
+            q_rows[group, row:row + both, HD:] = jnp.broadcast_to(
                 bias_by_head[pl.ds(core * heads + h, 1), :], (both, HD)
             ).astype(jnp.bfloat16)
+        for group in range(groups):
+            q_ext[group] = q_rows[group].T
 
     keys_here = 4 * both
-    cuts = [slice(i * HD, (i + 1) * HD) for i in range(keys_here // HD)]
-    factor = LOG2E / math.sqrt(HD)
+    scale = 1.0 / math.sqrt(HD)
+    chunks = [slice(i, min(i + 2 * HD, rows)) for i in range(0, rows, 2 * HD)]
 
     def attend(k, group):
         @pl.when(z >= k)
@@ -375,37 +376,28 @@
             onehot = jnp.where(block_of == key_lane, 1.0, 0.0).astype(jnp.bfloat16)
             cols = slice(group * HD, (group + 1) * HD)
             key = k_all[pl.ds(plane * 4, 4), :, cols].reshape(keys_here, HD)
-            value = v_all[pl.ds(plane * 4, 4), :, cols].reshape(keys_here, HD)
-            s = lax.dot_general(
-                q_ext[group],
-                jnp.concatenate([key, onehot], axis=1),
-                (((1,), (1,)), ((), ())),
-                preferred_element_type=jnp.float32,
-            )
-            if k == 0:
-                row_pos = chip * both + lax.broadcasted_iota(jnp.int32, s.shape, 0) % both
-                col_pos = lax.broadcasted_iota(jnp.int32, s.shape, 1)
-                s = jnp.where(col_pos <= row_pos, s, MASKED)
-            high = s[:, cuts[0]]
-            for cut in cuts[1:]:
-                high = jnp.maximum(high, s[:, cut])
-            high = jnp.broadcast_to(jnp.max(high, axis=1, keepdims=True), (rows, HD))
-            if k > 0:
-                old = top[group]
-                high = jnp.maximum(high, old)
-                shrink = jnp.exp2((old - high) * factor)
-            parts = [jnp.exp2((s[:, cut] - high) * factor) for cut in cuts]
-            w = jnp.concatenate([part.astype(jnp.bfloat16) for part in parts], axis=1)
-            part = parts[0]
-            for more in parts[1:]:
-                part = part + more
-            mixed = jnp.dot(w, value, preferred_element_type=jnp.float32)
-            if k > 0:
-                part = part + total[group] * shrink
-                mixed = mixed + acc[group] * shrink
-            top[group] = high
-            total[group] = part
-            acc[group] = mixed
+            value = v_all[pl.ds(plane * 4, 4), :, cols].reshape(keys_here, HD).T
+            key = jnp.concatenate([key, onehot], axis=1)
+            for chunk in chunks:
+                s = jnp.dot(key, q_ext[group, :, chunk], preferred_element_type=jnp.float32)
+                if k == 0:
+                    row_pos = chip * both + lax.broadcasted_iota(jnp.int32, s.shape, 1) % both
+                    key_pos = lax.broadcasted_iota(jnp.int32, s.shape, 0)
+                    s = jnp.where(key_pos <= row_pos, s, MASKED)
+                high = jnp.max(s, axis=0, keepdims=True)
+                if k > 0:
+                    old = top[group, :, chunk]
+                    high = jnp.maximum(high, old)
+                    shrink = jnp.exp((old - high) * scale)
+                w = jnp.exp((s - high) * scale)
+                part = jnp.sum(w, axis=0, keepdims=True)
+                mixed = jnp.dot(value, w.astype(jnp.bfloat16), preferred_element_type=jnp.float32)
+                if k > 0:
+                    part = part + total[group, :, chunk] * shrink
+                    mixed = mixed + acc[group, :, chunk] * shrink
+                top[group, :, chunk] = high
+                total[group, :, chunk] = part
+                acc[group, :, chunk] = mixed
 
     own_pieces()
     q_swap.start()
@@ -426,8 +418,7 @@
     mine = pl.ds(core * heads, heads)
     home = swap(leaving, done.at[mine], 1)
     for group in range(groups):
-        summed = jnp.sum(total[group], axis=1, keepdims=True)
-        result = (acc[group] / summed).astype(jnp.bfloat16)
+        result = (acc[group] / total[group]).T.astype(jnp.bfloat16)
         result = result.reshape(per_group, 2, tokens, HD)
         here = jnp.where(core == 0, result[:, 0], result[:, 1])
         there = jnp.where(core == 0, result[:, 1], result[:, 0])
@@ -449,20 +440,21 @@
     rows = H // KVH * 2 * tokens
     groups = KVH // 2
     table = block_index.transpose(0, 2, 1)
-    any_spec = pl.BlockSpec(memory_space=pl.ANY)
+    hbm_spec = pl.BlockSpec(memory_space=pltpu.HBM)
     return pl.pallas_call(
         plane_kernel,
         out_shape=jax.ShapeDtypeStruct(queries.shape, jnp.bfloat16),
-        in_specs=[any_spec] * 4 + [pl.BlockSpec(memory_space=pltpu.SMEM)],
+        in_specs=[hbm_spec] * 4 + [pl.BlockSpec(memory_space=pltpu.SMEM)],
         out_specs=pl.BlockSpec(memory_space=pltpu.VMEM),
         scratch_shapes=[
             pltpu.VMEM((planes * 4, 2 * tokens, groups * HD), jnp.bfloat16),
             pltpu.VMEM((planes * 4, 2 * tokens, groups * HD), jnp.bfloat16),
             pltpu.VMEM((2, tokens, H // 2 * HD), jnp.bfloat16),
             pltpu.VMEM((groups, rows, 2 * HD), jnp.bfloat16),
-            pltpu.VMEM((groups, rows, HD), jnp.float32),
-            pltpu.VMEM((groups, rows, HD), jnp.float32),
-            pltpu.VMEM((groups, rows, HD), jnp.float32),
+            pltpu.VMEM((groups, 2 * HD, rows), jnp.bfloat16),
+            pltpu.VMEM((groups, HD, rows), jnp.float32),
+            pltpu.VMEM((groups, 1, rows), jnp.float32),
+            pltpu.VMEM((groups, 1, rows), jnp.float32),
             pltpu.VMEM(table.shape[1:], jnp.int32),
             pltpu.VMEM((HD, HD), jnp.float32),
             pltpu.VMEM((HD, HD), jnp.float32),
@@ -475,7 +467,7 @@
             pltpu.SemaphoreType.DMA((planes, 4, 2, 2)),
         ],
         compiler_params=pltpu.CompilerParams(
-            collective_id=0, has_side_effects=True, vmem_limit_bytes=60 * 1024 * 1024
+            collective_id=0, has_side_effects=True, vmem_limit_bytes=40 * 1024 * 1024
         ),
     )(queries, keys, values, table, head_order)
 

time: 35.1 us -> 39.1 us (1.11)
  local copies, waits for them, and re-layouts: 1.82 us -> 5.02 us
  Pallas kernels: 33.1 us -> 33.8 us
    unnamed x1 -> x11, local copies, waits for them, and re-layouts: 1.82 us -> 5.02 us
    pallas_call x1, Pallas kernels: 33.1 us -> 33.8 us  [planes_local(): pl.pallas_call(plane_kernel, out_shape=jax.ShapeDtypeStruct(queries.shape...]
where the time goes in v3:
time: 39.1 us; the launch traced here: 38.9 us
  Pallas kernels  33.8 us (86%)
  local copies, waits for them, and re-layouts  5.02 us (13%)
    pallas_call x1, Pallas kernels, planes_local(): pl.pallas_call(plane_kernel, out_shape=jax.ShapeDtypeStruct(queries.shape...  33.8 us
    unnamed x11, local copies, waits for them, and re-layouts  5.02 us

profile of v3, /device:TPU:25, one launch (start us, length us, event | category | flops | bytes accessed | tf_op | source)
XLA Modules:
  0.0 38.9 jit_solution(15617263499983764160)
XLA Ops:
  0.0 0.0 copy-start.4
  0.0 0.7 %copy-done.4 = s32[28]{0:T(128)S(1)} copy-done((s32[28]{0:T(128)S(1)}, s32[28]{0:T(128)}, u32[]{:S(2)}) %copy-start.4) | copy-done | bytes 136
  0.7 0.0 copy-start
  0.7 1.0 %copy-done = bf16[64,3584]{1,0:T(8,128)(2,1)S(1)} copy-done((bf16[64,3584]{1,0:T(8,128)(2,1)S(1)}, bf16[64,3584]{1,0:T(8,128)(2,1)}, u32[]{:S(2)}) %copy-start) | copy-done | bytes 458776
  1.7 0.0 copy-start.1
  1.7 0.9 %copy-done.1 = s32[16,28,16]{1,2,0:T(8,128)S(1)} copy-done((s32[16,28,16]{1,2,0:T(8,128)S(1)}, s32[16,28,16]{1,2,0:T(8,128)}, u32[]{:S(2)}) %copy-start.1) | copy-done | bytes 28696
  2.6 0.0 copy-start.2
  2.6 0.8 %copy-done.2 = bf16[64,512]{1,0:T(8,128)(2,1)S(1)} copy-done((bf16[64,512]{1,0:T(8,128)(2,1)S(1)}, bf16[64,512]{1,0:T(8,128)(2,1)}, u32[]{:S(2)}) %copy-start.2) | copy-done | bytes 65560
  3.4 0.0 copy-start.3
  3.4 0.8 %copy-done.3 = bf16[64,512]{1,0:T(8,128)(2,1)S(1)} copy-done((bf16[64,512]{1,0:T(8,128)(2,1)S(1)}, bf16[64,512]{1,0:T(8,128)(2,1)}, u32[]{:S(2)}) %copy-start.3) | copy-done | bytes 65560
  4.3 33.8 %shard_map.55 = bf16[64,3584]{1,0:T(8,128)(2,1)S(1)} custom-call(bf16[64,3584]{1,0:T(8,128)(2,1)S(1)} %copy-done, bf16[64,512]{1,0:T(8,128)(2,1)S(1)} %copy-done.2, bf16[64,512]{1,0:T(8,128)(2,1)S(1)} %copy-done.3, s32[16,16,28]{2,1,0:T(8,128)S(1)} %bitcast.1, s32[28]{0:T(128)S(1)} %copy-done.4), custom_call_target="tpu_custom_call" | custom-call | tf_op jit(solution)/shard_map/pallas_call | solution.py:444
  38.1 0.8 %copy.7 = bf16[64,3584]{1,0:T(8,128)(2,1)} copy(bf16[64,3584]{1,0:T(8,128)(2,1)S(1)} %shard_map.55) | data formatting | bytes 917504
Async XLA Ops:
  0.0 0.7 %copy-start.4 = (s32[28]{0:T(128)S(1)}, s32[28]{0:T(128)}, u32[]{:S(2)}) copy-start(s32[28]{0:T(128)} %order_ref.1) | copy-start | bytes 340
  0.7 1.0 %copy-start = (bf16[64,3584]{1,0:T(8,128)(2,1)S(1)}, bf16[64,3584]{1,0:T(8,128)(2,1)}, u32[]{:S(2)}) copy-start(bf16[64,3584]{1,0:T(8,128)(2,1)} %q_ref.1) | copy-start | bytes 1376260
  1.7 0.9 %copy-start.1 = (s32[16,28,16]{1,2,0:T(8,128)S(1)}, s32[16,28,16]{1,2,0:T(8,128)}, u32[]{:S(2)}) copy-start(s32[16,28,16]{1,2,0:T(8,128)} %param.9) | copy-start | bytes 86020
  2.6 0.8 %copy-start.2 = (bf16[64,512]{1,0:T(8,128)(2,1)S(1)}, bf16[64,512]{1,0:T(8,128)(2,1)}, u32[]{:S(2)}) copy-start(bf16[64,512]{1,0:T(8,128)(2,1)} %k_ref.1) | copy-start | bytes 196612
  3.4 0.8 %copy-start.3 = (bf16[64,512]{1,0:T(8,128)(2,1)S(1)}, bf16[64,512]{1,0:T(8,128)(2,1)}, u32[]{:S(2)}) copy-start(bf16[64,512]{1,0:T(8,128)(2,1)} %v_ref.1) | copy-start | bytes 196612

commit v4 on v0

--- a/solution.py
+++ b/solution.py
@@ -4,6 +4,8 @@
 import jax
 import jax.numpy as jnp
 from jax import lax
+from jax.experimental import pallas as pl
+from jax.experimental.pallas import tpu as pltpu
 from jax.sharding import PartitionSpec as P
 
 H = 28
@@ -13,6 +15,7 @@
 
 
 FLOOR = -1e30
+MESH = pl.DeviceIdType.MESH
 
 
 def positions(stripes, stripe_len, device, ctx_total):
@@ -130,9 +133,353 @@
     return returned.reshape(local_tokens, H * HD)
 
 
+MASKED = -1e30
+
+
+def plane_kernel(
+    q_ref, k_ref, v_ref, table_ref, order_ref, out_ref,
+    k_all, v_all, q_in, q_rows, q_ext, acc, top, total, lists, bias_by_block,
+    bias_by_head, done, leaving, local_sems, piece_send, piece_recv, head_send, head_recv,
+    send_sems, recv_sems,
+):
+    z = lax.axis_index("head")
+    ctx = lax.axis_index("ctx")
+    planes = lax.axis_size("head")
+    tokens = q_ref.shape[0]
+    per_group = H // KVH
+    width = per_group * HD
+    rows = 4 * per_group * tokens
+    lane_keys = 4 * tokens
+    core = ctx % 2
+    other = 1 - core
+    chip = ctx // 2
+    x_chip = chip + 1 - 2 * (chip % 2)
+    y_chip = chip + 2 - 4 * (chip // 2)
+    d_chip = x_chip + y_chip - chip
+    away = (d_chip, x_chip, y_chip)
+    sib = 2 * chip + other
+    bufs = (k_all, v_all)
+    heres = (k_ref, v_ref)
+
+    def head_columns(of_chip, size):
+        return pl.ds(pl.multiple_of(of_chip * size, size), size)
+
+    def chip_rows(of_chip):
+        return pl.ds(pl.multiple_of(of_chip * tokens, tokens), tokens)
+
+    own_places = [bufs[which].at[z * 2 + core, chip_rows(chip)] for which in (0, 1)]
+    local_copies = [
+        pltpu.make_async_copy(
+            heres[which].at[:, head_columns(chip, HD)], own_places[which], local_sems.at[which]
+        )
+        for which in (0, 1)
+    ]
+    local_copies.append(pltpu.make_async_copy(
+        q_ref.at[:, head_columns(chip, width)], q_in.at[3], local_sems.at[2]
+    ))
+    local_copies.append(pltpu.make_async_copy(
+        table_ref.at[pl.ds(z * 4, 4)], lists, local_sems.at[3]
+    ))
+    for copy in local_copies:
+        copy.start()
+
+    barrier = pltpu.get_barrier_semaphore()
+
+    def greet(head_to, ctx_to):
+        pl.semaphore_signal(
+            barrier, inc=1, device_id={"head": head_to, "ctx": ctx_to}, device_id_type=MESH
+        )
+
+    greet(z, sib)
+    for near in away:
+        greet(z, 2 * near + core)
+
+    @pl.when(z > 0)
+    def _():
+        greet(z - 1, ctx)
+
+    @pl.when(z < planes - 1)
+    def _():
+        greet(z + 1, ctx)
+
+    pl.semaphore_wait(
+        barrier, 4 + (z > 0).astype(jnp.int32) + (z < planes - 1).astype(jnp.int32)
+    )
+
+    def remote(src, dst, send_sem, recv_sem, head_to, ctx_to):
+        return pltpu.make_async_remote_copy(
+            src_ref=src,
+            dst_ref=dst,
+            send_sem=send_sem,
+            recv_sem=recv_sem,
+            device_id={"head": head_to, "ctx": ctx_to},
+            device_id_type=MESH,
+        )
+
+    def piece(which, r):
+        return remote(
+            heres[which].at[:, head_columns(away[r], HD)],
+            own_places[which],
+            piece_send.at[which, r],
+            piece_recv.at[which, r],
+            z, 2 * away[r] + core,
+        )
+
+    def piece_arrived(which, r):
+        place = bufs[which].at[z * 2 + core, chip_rows(away[r])]
+        remote(
+            place, place, piece_send.at[which, r], piece_recv.at[which, r], z, sib
+        ).wait_recv()
+
+    def queries_out(r):
+        return remote(
+            q_ref.at[:, head_columns(away[r], width)],
+            q_in.at[r],
+            head_send.at[0, r],
+            head_recv.at[0, r],
+            z, 2 * away[r] + core,
+        )
+
+    def result_home(r):
+        return remote(
+            leaving.at[r],
+            done.at[pl.ds(chip * per_group, per_group)],
+            head_send.at[1, r],
+            head_recv.at[1, r],
+            z, 2 * away[r] + core,
+        )
+
+    def result_arrived(r):
+        remote(
+            leaving.at[r],
+            done.at[pl.ds(away[r] * per_group, per_group)],
+            head_send.at[1, r],
+            head_recv.at[1, r],
+            z, sib,
+        ).wait_recv()
+
+    def whole(which, k, lane, kind, head_to, ctx_to):
+        place = bufs[which].at[(z - k) * 2 + lane]
+        return remote(
+            place, place, send_sems.at[k, kind], recv_sems.at[z - k, lane, which],
+            head_to, ctx_to,
+        )
+
+    def column(k):
+        @pl.when(z >= k)
+        def _():
+            for which in (0, 1):
+                if k == 0:
+                    local_copies[which].wait()
+                    for r in range(3):
+                        piece_arrived(which, r)
+                else:
+                    whole(which, k, core, 0, z, sib).wait_recv()
+
+                @pl.when(z < planes - 1)
+                def _():
+                    whole(which, k, core, which, z + 1, ctx).start()
+
+                whole(which, k, core, 2 + which, z, sib).start()
+
+    def beside(k):
+        @pl.when(z >= k)
+        def _():
+            for which in (0, 1):
+                whole(which, k, other, 0, z, sib).wait_recv()
+
+    def sent(k):
+        @pl.when(z >= k)
+        def _():
+            @pl.when(z < planes - 1)
+            def _():
+                for kind in (0, 1):
+                    whole(0, k, core, kind, z, sib).wait_send()
+
+            for kind in (2, 3):
+                whole(0, k, core, kind, z, sib).wait_send()
+
+    def prepare_bias():
+        local_copies[3].wait()
+        listed = lists[...]
+        entries = listed.shape[1]
+        spot = lax.broadcasted_iota(jnp.int32, listed.shape, 1)
+        query_block = z * 4 + lax.broadcasted_iota(jnp.int32, listed.shape, 0)
+        last = jnp.min(jnp.where(listed == query_block, spot, entries), axis=1, keepdims=True)
+        listed = jnp.where(spot <= last, listed, -1)
+        bias_by_block[...] = jnp.zeros_like(bias_by_block)
+        for chip_here in range(4):
+            block = lax.broadcasted_iota(jnp.int32, (entries, H), 0)
+            bias = jnp.full((entries, H), MASKED, jnp.float32)
+            for e in range(entries):
+                bias = jnp.where(listed[chip_here, e:e + 1, :] == block, 0.0, bias)
+            bias_by_block[:entries, :H] = bias
+            bias_by_head[chip_here] = bias_by_block[...].T
+
+    def prepare_rows(r, of_chip):
+        for g in range(per_group):
+            row = (r * per_group + g) * tokens
+            q_rows[row:row + tokens, :HD] = q_in[r, :, g * HD:(g + 1) * HD]
+            q_rows[row:row + tokens, HD:] = jnp.broadcast_to(
+                bias_by_head[of_chip, pl.ds(chip * per_group + g, 1), :], (tokens, HD)
+            ).astype(jnp.bfloat16)
+
+    keys_here = 2 * lane_keys
+    half_rows = rows // 2
+    scale = 1.0 / math.sqrt(HD)
+    starts = range(0, half_rows, 2 * HD)
+    chunks = [
+        [slice(h * half_rows + i, h * half_rows + min(i + 2 * HD, half_rows)) for i in starts]
+        for h in (0, 1)
+    ]
+
+    def attend(k, half):
+        @pl.when(z >= k)
+        def _():
+            plane = z - k
+            key_row = lax.broadcasted_iota(jnp.int32, (keys_here, HD), 0)
+            key_lane = lax.broadcasted_iota(jnp.int32, (keys_here, HD), 1)
+            block_of = plane * 4 + key_row % lane_keys // tokens
+            onehot = jnp.where(block_of == key_lane, 1.0, 0.0).astype(jnp.bfloat16)
+            key = k_all[pl.ds(plane * 2, 2)].reshape(keys_here, HD)
+            value = v_all[pl.ds(plane * 2, 2)].reshape(keys_here, HD).T
+            key = jnp.concatenate([key, onehot], axis=1)
+            for chunk in chunks[half]:
+                s = jnp.dot(key, q_ext[:, chunk], preferred_element_type=jnp.float32)
+                if k == 0:
+                    key_at = lax.broadcasted_iota(jnp.int32, (keys_here, 1), 0)
+                    key_pos = (
+                        key_at % lane_keys // tokens * 2 + key_at // lane_keys
+                    ) * tokens + key_at % tokens
+                    row_at = chunk.start + lax.broadcasted_iota(
+                        jnp.int32, (1, chunk.stop - chunk.start), 1
+                    )
+                    source = row_at // (per_group * tokens)
+                    row_chip = jnp.where(
+                        source == 0, d_chip,
+                        jnp.where(source == 1, x_chip, jnp.where(source == 2, y_chip, chip)),
+                    )
+                    row_pos = (row_chip * 2 + core) * tokens + row_at % tokens
+                    s = jnp.where(key_pos <= row_pos, s, MASKED)
+                high = jnp.max(s, axis=0, keepdims=True)
+                if k > 0:
+                    old = top[:, chunk]
+                    high = jnp.maximum(high, old)
+                    shrink = jnp.exp((old - high) * scale)
+                w = jnp.exp((s - high) * scale)
+                part = jnp.sum(w, axis=0, keepdims=True)
+                mixed = jnp.dot(value, w.astype(jnp.bfloat16), preferred_element_type=jnp.float32)
+                if k > 0:
+                    part = part + total[:, chunk] * shrink
+                    mixed = mixed + acc[:, chunk] * shrink
+                top[:, chunk] = high
+                total[:, chunk] = part
+                acc[:, chunk] = mixed
+
+    def finish(half):
+        part = slice(half * half_rows, (half + 1) * half_rows)
+        result = (acc[:, part] / total[:, part]).T.astype(jnp.bfloat16)
+        leaving[2 * half:2 * half + 2] = result.reshape(2, per_group, tokens, HD)
+
+    for which in (0, 1):
+        for r in range(3):
+            piece(which, r).start()
+    for r in range(3):
+        queries_out(r).start()
+    prepare_bias()
+    column(0)
+    local_copies[2].wait()
+    prepare_rows(3, chip)
+    for r in range(3):
+        queries_out(r).wait_recv()
+        prepare_rows(r, away[r])
+    q_ext[...] = q_rows[...].T
+    column(1)
+    beside(0)
+    mine = pl.ds(chip * per_group, per_group)
+    keep = pltpu.make_async_copy(leaving.at[3], done.at[mine], local_sems.at[4])
+    for k in range(4):
+        attend(k, 0)
+        if k < 2:
+            column(k + 2)
+
+        @pl.when(z == k)
+        def _():
+            finish(0)
+            result_home(0).start()
+            result_home(1).start()
+
+        attend(k, 1)
+
+        @pl.when(z == k)
+        def _():
+            finish(1)
+            result_home(2).start()
+            keep.start()
+
+        if k < 3:
+            beside(k + 1)
+
+    for which in (0, 1):
+        for r in range(3):
+            piece(which, r).wait_send()
+    for r in range(3):
+        queries_out(r).wait_send()
+    for k in range(4):
+        sent(k)
+    keep.wait()
+    for r in range(3):
+        result_arrived(r)
+    for place in range(H):
+        out_ref[:, place * HD:(place + 1) * HD] = done[order_ref[place]]
+    for r in range(3):
+        result_home(r).wait_send()
+
+
+def planes_local(queries, keys, values, block_index, block_count, head_order):
+    tokens = queries.shape[0]
+    planes = lax.axis_size("head")
+    per_group = H // KVH
+    rows = 4 * per_group * tokens
+    table = block_index.transpose(0, 2, 1)
+    any_spec = pl.BlockSpec(memory_space=pl.ANY)
+    return pl.pallas_call(
+        plane_kernel,
+        out_shape=jax.ShapeDtypeStruct(queries.shape, jnp.bfloat16),
+        in_specs=[any_spec] * 4 + [pl.BlockSpec(memory_space=pltpu.SMEM)],
+        out_specs=pl.BlockSpec(memory_space=pltpu.VMEM),
+        scratch_shapes=[
+            pltpu.VMEM((planes * 2, 4 * tokens, HD), jnp.bfloat16),
+            pltpu.VMEM((planes * 2, 4 * tokens, HD), jnp.bfloat16),
+            pltpu.VMEM((4, tokens, per_group * HD), jnp.bfloat16),
+            pltpu.VMEM((rows, 2 * HD), jnp.bfloat16),
+            pltpu.VMEM((2 * HD, rows), jnp.bfloat16),
+            pltpu.VMEM((HD, rows), jnp.float32),
+            pltpu.VMEM((1, rows), jnp.float32),
+            pltpu.VMEM((1, rows), jnp.float32),
+            pltpu.VMEM((4,) + table.shape[1:], jnp.int32),
+            pltpu.VMEM((HD, HD), jnp.float32),
+            pltpu.VMEM((4, HD, HD), jnp.float32),
+            pltpu.VMEM((H, tokens, HD), jnp.bfloat16),
+            pltpu.VMEM((4, per_group, tokens, HD), jnp.bfloat16),
+            pltpu.SemaphoreType.DMA((5,)),
+            pltpu.SemaphoreType.DMA((2, 3)),
+            pltpu.SemaphoreType.DMA((2, 3)),
+            pltpu.SemaphoreType.DMA((2, 3)),
+            pltpu.SemaphoreType.DMA((2, 3)),
+            pltpu.SemaphoreType.DMA((planes, 4)),
+            pltpu.SemaphoreType.DMA((planes, 2, 2)),
+        ],
+        compiler_params=pltpu.CompilerParams(
+            collective_id=0, has_side_effects=True, vmem_limit_bytes=60 * 1024 * 1024
+        ),
+    )(queries, keys, values, table, head_order)
+
+
 def solution(mesh):
+    in_planes = mesh.shape["head"] == 4 and mesh.shape["ctx"] == 8
     return jax.shard_map(
-        local,
+        planes_local if in_planes else local,
         mesh=mesh,
         in_specs=(
             P(("head", "ctx"), None),

time: 164 us -> 36.6 us (0.22)
  the two profiles are of different devices: /device:TPU:0 before, /device:TPU:24 now
where the time goes in v4:
time: 36.6 us; the launch traced here: 36.4 us
  Pallas kernels  34.6 us (95%)
  local copies, waits for them, and re-layouts  1.82 us (5%)
    pallas_call x1, Pallas kernels, planes_local(): pl.pallas_call(plane_kernel, out_shape=jax.ShapeDtypeStruct(queries.shape...  34.6 us
    unnamed x1, local copies, waits for them, and re-layouts  1.82 us

profile of v4, /device:TPU:24, one launch (start us, length us, event | category | flops | bytes accessed | tf_op | source)
XLA Modules:
  0.0 36.4 jit_solution(760023163894835034)
XLA Ops:
  0.0 34.6 %shard_map.55 = bf16[64,3584]{1,0:T(8,128)(2,1)} custom-call(bf16[64,3584]{1,0:T(8,128)(2,1)} %q_ref.1, bf16[64,512]{1,0:T(8,128)(2,1)} %k_ref.1, bf16[64,512]{1,0:T(8,128)(2,1)} %v_ref.1, s32[16,16,28]{2,1,0:T(8,128)} %bitcast.1, s32[28]{0:T(128)} %order_ref.1), custom_call_target="tpu_custom_call" | custom-call | tf_op jit(solution)/shard_map/pallas_call | solution.py:446
  34.6 1.8 %copy.7 = bf16[64,3584]{1,0:T(8,128)(2,1)} copy(bf16[64,3584]{1,0:T(8,128)(2,1)} %shard_map.55) | data formatting | bytes 917504

commit v5 on v4

--- a/solution.py
+++ b/solution.py
@@ -156,7 +156,8 @@
     x_chip = chip + 1 - 2 * (chip % 2)
     y_chip = chip + 2 - 4 * (chip // 2)
     d_chip = x_chip + y_chip - chip
-    away = (d_chip, x_chip, y_chip)
+    away = (y_chip, x_chip, d_chip)
+    slots = (0, 2, 3)
     sib = 2 * chip + other
     bufs = (k_all, v_all)
     heres = (k_ref, v_ref)
@@ -175,7 +176,7 @@
         for which in (0, 1)
     ]
     local_copies.append(pltpu.make_async_copy(
-        q_ref.at[:, head_columns(chip, width)], q_in.at[3], local_sems.at[2]
+        q_ref.at[:, head_columns(chip, width)], q_in.at[1], local_sems.at[2]
     ))
     local_copies.append(pltpu.make_async_copy(
         table_ref.at[pl.ds(z * 4, 4)], lists, local_sems.at[3]
@@ -234,7 +235,7 @@
     def queries_out(r):
         return remote(
             q_ref.at[:, head_columns(away[r], width)],
-            q_in.at[r],
+            q_in.at[slots[r]],
             head_send.at[0, r],
             head_recv.at[0, r],
             z, 2 * away[r] + core,
@@ -242,7 +243,7 @@
 
     def result_home(r):
         return remote(
-            leaving.at[r],
+            leaving.at[slots[r]],
             done.at[pl.ds(chip * per_group, per_group)],
             head_send.at[1, r],
             head_recv.at[1, r],
@@ -251,7 +252,7 @@
 
     def result_arrived(r):
         remote(
-            leaving.at[r],
+            leaving.at[slots[r]],
             done.at[pl.ds(away[r] * per_group, per_group)],
             head_send.at[1, r],
             head_recv.at[1, r],
@@ -356,8 +357,8 @@
                     )
                     source = row_at // (per_group * tokens)
                     row_chip = jnp.where(
-                        source == 0, d_chip,
-                        jnp.where(source == 1, x_chip, jnp.where(source == 2, y_chip, chip)),
+                        source == 0, y_chip,
+                        jnp.where(source == 1, chip, jnp.where(source == 2, x_chip, d_chip)),
                     )
                     row_pos = (row_chip * 2 + core) * tokens + row_at % tokens
                     s = jnp.where(key_pos <= row_pos, s, MASKED)
@@ -381,44 +382,68 @@
         result = (acc[:, part] / total[:, part]).T.astype(jnp.bfloat16)
         leaving[2 * half:2 * half + 2] = result.reshape(2, per_group, tokens, HD)
 
+    mine = pl.ds(chip * per_group, per_group)
+    keep = pltpu.make_async_copy(leaving.at[1], done.at[mine], local_sems.at[4])
+
+    def turn_rows(half):
+        part = slice(half * half_rows, (half + 1) * half_rows)
+        q_ext[:, part] = q_rows[part, :].T
+
+    def send_half(half):
+        if half == 0:
+            result_home(0).start()
+            keep.start()
+        else:
+            result_home(2).start()
+            result_home(1).start()
+
     for which in (0, 1):
         for r in range(3):
             piece(which, r).start()
-    for r in range(3):
+    prepare_bias()
+    for r in (2, 0, 1):
         queries_out(r).start()
-    prepare_bias()
     column(0)
     local_copies[2].wait()
-    prepare_rows(3, chip)
-    for r in range(3):
-        queries_out(r).wait_recv()
-        prepare_rows(r, away[r])
-    q_ext[...] = q_rows[...].T
+    prepare_rows(1, chip)
+    queries_out(0).wait_recv()
+    prepare_rows(0, y_chip)
+    turn_rows(0)
     column(1)
     beside(0)
-    mine = pl.ds(chip * per_group, per_group)
-    keep = pltpu.make_async_copy(leaving.at[3], done.at[mine], local_sems.at[4])
-    for k in range(4):
+    attend(0, 0)
+    for r in (1, 2):
+        queries_out(r).wait_recv()
+        prepare_rows(slots[r], away[r])
+    turn_rows(1)
+    attend(0, 1)
+
+    @pl.when(z == 0)
+    def _():
+        finish(0)
+        finish(1)
+        send_half(1)
+        send_half(0)
+
+    for k in range(1, 4):
+        if k == 1:
+            column(2)
+        beside(k)
+        attend(k, 1)
+        if k == 2:
+            column(3)
+
+        @pl.when(z == k)
+        def _():
+            finish(1)
+            send_half(1)
+
         attend(k, 0)
-        if k < 2:
-            column(k + 2)
 
         @pl.when(z == k)
         def _():
             finish(0)
-            result_home(0).start()
-            result_home(1).start()
-
-        attend(k, 1)
-
-        @pl.when(z == k)
-        def _():
-            finish(1)
-            result_home(2).start()
-            keep.start()
-
-        if k < 3:
-            beside(k + 1)
+            send_half(0)
 
     for which in (0, 1):
         for r in range(3):

time: 36.6 us -> 35.2 us (0.962)
  the two profiles are of different devices: /device:TPU:24 before, /device:TPU:25 now
where the time goes in v5:
time: 35.2 us; the launch traced here: 34.9 us
  Pallas kernels  33 us (94%)
  local copies, waits for them, and re-layouts  1.82 us (5%)
    pallas_call x1, Pallas kernels, planes_local(): pl.pallas_call(plane_kernel, out_shape=jax.ShapeDtypeStruct(queries.shape...  33 us
    unnamed x1, local copies, waits for them, and re-layouts  1.82 us

profile of v5, /device:TPU:25, one launch (start us, length us, event | category | flops | bytes accessed | tf_op | source)
XLA Modules:
  0.0 34.9 jit_solution(13360417945033193402)
XLA Ops:
  0.0 33.0 %shard_map.55 = bf16[64,3584]{1,0:T(8,128)(2,1)} custom-call(bf16[64,3584]{1,0:T(8,128)(2,1)} %q_ref.1, bf16[64,512]{1,0:T(8,128)(2,1)} %k_ref.1, bf16[64,512]{1,0:T(8,128)(2,1)} %v_ref.1, s32[16,16,28]{2,1,0:T(8,128)} %bitcast.1, s32[28]{0:T(128)} %order_ref.1), custom_call_target="tpu_custom_call" | custom-call | tf_op jit(solution)/shard_map/pallas_call | solution.py:471
  33.0 1.8 %copy.7 = bf16[64,3584]{1,0:T(8,128)(2,1)} copy(bf16[64,3584]{1,0:T(8,128)(2,1)} %shard_map.55) | data formatting | bytes 917504

commit v6 on v5

--- a/solution.py
+++ b/solution.py
@@ -334,7 +334,7 @@
         for h in (0, 1)
     ]
 
-    def attend(k, half):
+    def attend(k, halves):
         @pl.when(z >= k)
         def _():
             plane = z - k
@@ -345,8 +345,12 @@
             key = k_all[pl.ds(plane * 2, 2)].reshape(keys_here, HD)
             value = v_all[pl.ds(plane * 2, 2)].reshape(keys_here, HD).T
             key = jnp.concatenate([key, onehot], axis=1)
-            for chunk in chunks[half]:
-                s = jnp.dot(key, q_ext[:, chunk], preferred_element_type=jnp.float32)
+            todo = [chunk for half in halves for chunk in chunks[half]]
+
+            def score(chunk):
+                return jnp.dot(key, q_ext[:, chunk], preferred_element_type=jnp.float32)
+
+            def weigh(chunk, s):
                 if k == 0:
                     key_at = lax.broadcasted_iota(jnp.int32, (keys_here, 1), 0)
                     key_pos = (
@@ -363,19 +367,34 @@
                     row_pos = (row_chip * 2 + core) * tokens + row_at % tokens
                     s = jnp.where(key_pos <= row_pos, s, MASKED)
                 high = jnp.max(s, axis=0, keepdims=True)
+                shrink = None
                 if k > 0:
                     old = top[:, chunk]
                     high = jnp.maximum(high, old)
                     shrink = jnp.exp((old - high) * scale)
                 w = jnp.exp((s - high) * scale)
                 part = jnp.sum(w, axis=0, keepdims=True)
-                mixed = jnp.dot(value, w.astype(jnp.bfloat16), preferred_element_type=jnp.float32)
                 if k > 0:
                     part = part + total[:, chunk] * shrink
-                    mixed = mixed + acc[:, chunk] * shrink
                 top[:, chunk] = high
                 total[:, chunk] = part
+                return w.astype(jnp.bfloat16), shrink
+
+            def mix(chunk, w, shrink):
+                mixed = jnp.dot(value, w, preferred_element_type=jnp.float32)
+                if k > 0:
+                    mixed = mixed + acc[:, chunk] * shrink
                 acc[:, chunk] = mixed
+
+            scored = [score(chunk) for chunk in todo[:2]]
+            weighed = []
+            for i, chunk in enumerate(todo):
+                weighed.append(weigh(chunk, scored[i]))
+                if i + 2 < len(todo):
+                    scored.append(score(todo[i + 2]))
+                if i > 0:
+                    mix(todo[i - 1], *weighed[i - 1])
+            mix(todo[-1], *weighed[-1])
 
     def finish(half):
         part = slice(half * half_rows, (half + 1) * half_rows)
@@ -411,12 +430,12 @@
     turn_rows(0)
     column(1)
     beside(0)
-    attend(0, 0)
+    attend(0, (0,))
     for r in (1, 2):
         queries_out(r).wait_recv()
         prepare_rows(slots[r], away[r])
     turn_rows(1)
-    attend(0, 1)
+    attend(0, (1,))
 
     @pl.when(z == 0)
     def _():
@@ -429,21 +448,17 @@
         if k == 1:
             column(2)
         beside(k)
-        attend(k, 1)
-        if k == 2:
-            column(3)
+        attend(k, (1, 0))
 
         @pl.when(z == k)
         def _():
             finish(1)
             send_half(1)
-
-        attend(k, 0)
-
-        @pl.when(z == k)
-        def _():
             finish(0)
             send_half(0)
+
+        if k == 2:
+            column(3)
 
     for which in (0, 1):
         for r in range(3):

time: 35.2 us -> 32.4 us (0.920)
  Pallas kernels: 33 us -> 30.4 us
    pallas_call x1, Pallas kernels: 33 us -> 30.4 us  [planes_local(): pl.pallas_call(plane_kernel, out_shape=jax.ShapeDtypeStruct(queries.shape...]
where the time goes in v6:
time: 32.4 us; the launch traced here: 32.2 us
  Pallas kernels  30.4 us (94%)
  local copies, waits for them, and re-layouts  1.82 us (6%)
    pallas_call x1, Pallas kernels, planes_local(): pl.pallas_call(plane_kernel, out_shape=jax.ShapeDtypeStruct(queries.shape...  30.4 us
    unnamed x1, local copies, waits for them, and re-layouts  1.82 us

profile of v6, /device:TPU:25, one launch (start us, length us, event | category | flops | bytes accessed | tf_op | source)
XLA Modules:
  0.0 32.2 jit_solution(13890998776154760092)
XLA Ops:
  0.0 30.4 %shard_map.55 = bf16[64,3584]{1,0:T(8,128)(2,1)} custom-call(bf16[64,3584]{1,0:T(8,128)(2,1)} %q_ref.1, bf16[64,512]{1,0:T(8,128)(2,1)} %k_ref.1, bf16[64,512]{1,0:T(8,128)(2,1)} %v_ref.1, s32[16,16,28]{2,1,0:T(8,128)} %bitcast.1, s32[28]{0:T(128)} %order_ref.1), custom_call_target="tpu_custom_call" | custom-call | tf_op jit(solution)/shard_map/pallas_call | solution.py:486
  30.4 1.8 %copy.7 = bf16[64,3584]{1,0:T(8,128)(2,1)} copy(bf16[64,3584]{1,0:T(8,128)(2,1)} %shard_map.55) | data formatting | bytes 917504

commit v7 on v3

--- a/solution.py
+++ b/solution.py
@@ -137,9 +137,9 @@
 
 
 def plane_kernel(
-    q_ref, k_ref, v_ref, table_ref, order_ref, out_ref,
+    q_ref, k_ref, v_ref, table_ref, done,
     k_all, v_all, q_in, q_rows, q_ext, acc, top, total, lists, bias_by_block, bias_by_head,
-    done, leaving, local_sems, swap_send, swap_recv, send_sems, recv_sems,
+    staying, leaving, local_sems, swap_send, swap_recv, send_sems, recv_sems,
 ):
     z = lax.axis_index("head")
     ctx = lax.axis_index("ctx")
@@ -378,26 +378,44 @@
             key = k_all[pl.ds(plane * 4, 4), :, cols].reshape(keys_here, HD)
             value = v_all[pl.ds(plane * 4, 4), :, cols].reshape(keys_here, HD).T
             key = jnp.concatenate([key, onehot], axis=1)
-            for chunk in chunks:
-                s = jnp.dot(key, q_ext[group, :, chunk], preferred_element_type=jnp.float32)
+
+            def score(chunk):
+                return jnp.dot(key, q_ext[group, :, chunk], preferred_element_type=jnp.float32)
+
+            def weigh(chunk, s):
                 if k == 0:
                     row_pos = chip * both + lax.broadcasted_iota(jnp.int32, s.shape, 1) % both
                     key_pos = lax.broadcasted_iota(jnp.int32, s.shape, 0)
                     s = jnp.where(key_pos <= row_pos, s, MASKED)
                 high = jnp.max(s, axis=0, keepdims=True)
+                shrink = None
                 if k > 0:
                     old = top[group, :, chunk]
                     high = jnp.maximum(high, old)
                     shrink = jnp.exp((old - high) * scale)
                 w = jnp.exp((s - high) * scale)
                 part = jnp.sum(w, axis=0, keepdims=True)
-                mixed = jnp.dot(value, w.astype(jnp.bfloat16), preferred_element_type=jnp.float32)
                 if k > 0:
                     part = part + total[group, :, chunk] * shrink
-                    mixed = mixed + acc[group, :, chunk] * shrink
                 top[group, :, chunk] = high
                 total[group, :, chunk] = part
+                return w.astype(jnp.bfloat16), shrink
+
+            def mix(chunk, w, shrink):
+                mixed = jnp.dot(value, w, preferred_element_type=jnp.float32)
+                if k > 0:
+                    mixed = mixed + acc[group, :, chunk] * shrink
                 acc[group, :, chunk] = mixed
+
+            scored = [score(chunk) for chunk in chunks[:2]]
+            weighed = []
+            for i, chunk in enumerate(chunks):
+                weighed.append(weigh(chunk, scored[i]))
+                if i + 2 < len(chunks):
+                    scored.append(score(chunks[i + 2]))
+                if i > 0:
+                    mix(chunks[i - 1], *weighed[i - 1])
+            mix(chunks[-1], *weighed[-1])
 
     own_pieces()
     q_swap.start()
@@ -422,16 +440,32 @@
         result = result.reshape(per_group, 2, tokens, HD)
         here = jnp.where(core == 0, result[:, 0], result[:, 1])
         there = jnp.where(core == 0, result[:, 1], result[:, 0])
-        done[pl.ds(core * heads + group * per_group, per_group)] = here
+        staying[group * per_group:(group + 1) * per_group] = here
         leaving[group * per_group:(group + 1) * per_group] = there
     home.start()
+    keep = pltpu.make_async_copy(staying, done.at[mine], local_sems.at[4])
+    keep.start()
     for k in range(4):
         sent(k)
     q_swap.wait_send()
     swap(leaving, done.at[pl.ds(other * heads, heads)], 1).wait_recv()
-    for place in range(H):
-        out_ref[:, place * HD:(place + 1) * HD] = done[order_ref[place]]
+    keep.wait()
     home.wait_send()
+
+
+def order_kernel(done, order_ref, out_ref, sems):
+    copies = [
+        pltpu.make_async_copy(
+            done.at[order_ref[place]],
+            out_ref.at[:, place * HD:(place + 1) * HD],
+            sems.at[place],
+        )
+        for place in range(H)
+    ]
+    for copy in copies:
+        copy.start()
+    for copy in copies:
+        copy.wait()
 
 
 def planes_local(queries, keys, values, block_index, block_count, head_order):
@@ -440,12 +474,12 @@
     rows = H // KVH * 2 * tokens
     groups = KVH // 2
     table = block_index.transpose(0, 2, 1)
-    hbm_spec = pl.BlockSpec(memory_space=pltpu.HBM)
-    return pl.pallas_call(
+    any_spec = pl.BlockSpec(memory_space=pl.ANY)
+    attended = pl.pallas_call(
         plane_kernel,
-        out_shape=jax.ShapeDtypeStruct(queries.shape, jnp.bfloat16),
-        in_specs=[hbm_spec] * 4 + [pl.BlockSpec(memory_space=pltpu.SMEM)],
-        out_specs=pl.BlockSpec(memory_space=pltpu.VMEM),
+        out_shape=jax.ShapeDtypeStruct((H, tokens, HD), jnp.bfloat16),
+        in_specs=[any_spec] * 4,
+        out_specs=any_spec,
         scratch_shapes=[
             pltpu.VMEM((planes * 4, 2 * tokens, groups * HD), jnp.bfloat16),
             pltpu.VMEM((planes * 4, 2 * tokens, groups * HD), jnp.bfloat16),
@@ -458,18 +492,26 @@
             pltpu.VMEM(table.shape[1:], jnp.int32),
             pltpu.VMEM((HD, HD), jnp.float32),
             pltpu.VMEM((HD, HD), jnp.float32),
-            pltpu.VMEM((H, tokens, HD), jnp.bfloat16),
             pltpu.VMEM((H // 2, tokens, HD), jnp.bfloat16),
-            pltpu.SemaphoreType.DMA((4,)),
+            pltpu.VMEM((H // 2, tokens, HD), jnp.bfloat16),
+            pltpu.SemaphoreType.DMA((5,)),
             pltpu.SemaphoreType.DMA((2,)),
             pltpu.SemaphoreType.DMA((2,)),
             pltpu.SemaphoreType.DMA((planes, 16)),
             pltpu.SemaphoreType.DMA((planes, 4, 2, 2)),
         ],
         compiler_params=pltpu.CompilerParams(
-            collective_id=0, has_side_effects=True, vmem_limit_bytes=40 * 1024 * 1024
+            collective_id=0, has_side_effects=True, vmem_limit_bytes=60 * 1024 * 1024
         ),
-    )(queries, keys, values, table, head_order)
+    )(queries, keys, values, table)
+    return pl.pallas_call(
+        order_kernel,
+        out_shape=jax.ShapeDtypeStruct(queries.shape, jnp.bfloat16),
+        in_specs=[any_spec, pl.BlockSpec(memory_space=pltpu.SMEM)],
+        out_specs=any_spec,
+        scratch_shapes=[pltpu.SemaphoreType.DMA((H,))],
+        compiler_params=pltpu.CompilerParams(vmem_limit_bytes=60 * 1024 * 1024),
+    )(attended, head_order)
 
 
 def solution(mesh):

time: 39.1 us -> 47.9 us (1.23)
  Pallas kernels: 33.8 us -> 47.7 us
  local copies, waits for them, and re-layouts: 5.02 us -> 0 us
    pallas_call x1 -> x2, Pallas kernels: 33.8 us -> 47.7 us  [the longest x1 31.8 us: planes_local(): pl.pallas_call(plane_kernel, out_shape=jax.ShapeDtypeStruct((H, tokens, H...]
    unnamed x11 -> x0, local copies, waits for them, and re-layouts: 5.02 us -> none
where the time goes in v7:
time: 47.9 us; the launch traced here: 47.7 us
  Pallas kernels  47.7 us (100%)
    pallas_call x1, Pallas kernels, planes_local(): pl.pallas_call(plane_kernel, out_shape=jax.ShapeDtypeStruct((H, tokens, H...  31.8 us
    pallas_call x1, Pallas kernels, planes_local(): pl.pallas_call(order_kernel, out_shape=jax.ShapeDtypeStruct(queries.shape...  15.9 us

profile of v7, /device:TPU:25, one launch (start us, length us, event | category | flops | bytes accessed | tf_op | source)
XLA Modules:
  0.0 47.7 jit_solution(17871175907739040661)
XLA Ops:
  0.0 31.8 %shard_map.55.done = bf16[28,64,128]{2,1,0:T(8,128)(2,1)} custom-call(bf16[64,3584]{1,0:T(8,128)(2,1)} %q_ref.1, bf16[64,512]{1,0:T(8,128)(2,1)} %k_ref.1, bf16[64,512]{1,0:T(8,128)(2,1)} %v_ref.1, s32[16,16,28]{2,1,0:T(8,128)} %bitcast.1), custom_call_target="tpu_custom_call" | custom-call | tf_op jit(solution)/shard_map/pallas_call | solution.py:478
  31.8 15.9 %shard_map.56 = bf16[64,3584]{1,0:T(8,128)(2,1)} custom-call(bf16[28,64,128]{2,1,0:T(8,128)(2,1)} %shard_map.55.done, s32[28]{0:T(128)} %order_ref.1), custom_call_target="tpu_custom_call" | custom-call | tf_op jit(solution)/shard_map/pallas_call | solution.py:507

commit v8 on v6

--- a/solution.py
+++ b/solution.py
@@ -137,9 +137,9 @@
 
 
 def plane_kernel(
-    q_ref, k_ref, v_ref, table_ref, order_ref, out_ref,
+    q_ref, k_ref, v_ref, table_ref, done,
     k_all, v_all, q_in, q_rows, q_ext, acc, top, total, lists, bias_by_block,
-    bias_by_head, done, leaving, local_sems, piece_send, piece_recv, head_send, head_recv,
+    bias_by_head, leaving, local_sems, piece_send, piece_recv, head_send, head_recv,
     send_sems, recv_sems,
 ):
     z = lax.axis_index("head")
@@ -448,12 +448,21 @@
         if k == 1:
             column(2)
         beside(k)
-        attend(k, (1, 0))
+        if k < 3:
+            attend(k, (1, 0))
+        else:
+            attend(k, (1,))
 
         @pl.when(z == k)
         def _():
             finish(1)
             send_half(1)
+
+        if k == 3:
+            attend(k, (0,))
+
+        @pl.when(z == k)
+        def _():
             finish(0)
             send_half(0)
 
@@ -470,10 +479,13 @@
     keep.wait()
     for r in range(3):
         result_arrived(r)
+    for r in range(3):
+        result_home(r).wait_send()
+
+
+def order_kernel(done, order_ref, out_ref):
     for place in range(H):
         out_ref[:, place * HD:(place + 1) * HD] = done[order_ref[place]]
-    for r in range(3):
-        result_home(r).wait_send()
 
 
 def planes_local(queries, keys, values, block_index, block_count, head_order):
@@ -483,11 +495,11 @@
     rows = 4 * per_group * tokens
     table = block_index.transpose(0, 2, 1)
     any_spec = pl.BlockSpec(memory_space=pl.ANY)
-    return pl.pallas_call(
+    attended = pl.pallas_call(
         plane_kernel,
-        out_shape=jax.ShapeDtypeStruct(queries.shape, jnp.bfloat16),
-        in_specs=[any_spec] * 4 + [pl.BlockSpec(memory_space=pltpu.SMEM)],
-        out_specs=pl.BlockSpec(memory_space=pltpu.VMEM),
+        out_shape=jax.ShapeDtypeStruct((H, tokens, HD), jnp.bfloat16),
+        in_specs=[any_spec] * 4,
+        out_specs=any_spec,
         scratch_shapes=[
             pltpu.VMEM((planes * 2, 4 * tokens, HD), jnp.bfloat16),
             pltpu.VMEM((planes * 2, 4 * tokens, HD), jnp.bfloat16),
@@ -500,7 +512,6 @@
             pltpu.VMEM((4,) + table.shape[1:], jnp.int32),
             pltpu.VMEM((HD, HD), jnp.float32),
             pltpu.VMEM((4, HD, HD), jnp.float32),
-            pltpu.VMEM((H, tokens, HD), jnp.bfloat16),
             pltpu.VMEM((4, per_group, tokens, HD), jnp.bfloat16),
             pltpu.SemaphoreType.DMA((5,)),
             pltpu.SemaphoreType.DMA((2, 3)),
@@ -513,7 +524,16 @@
         compiler_params=pltpu.CompilerParams(
             collective_id=0, has_side_effects=True, vmem_limit_bytes=60 * 1024 * 1024
         ),
-    )(queries, keys, values, table, head_order)
+    )(queries, keys, values, table)
+    return pl.pallas_call(
+        order_kernel,
+        out_shape=jax.ShapeDtypeStruct(queries.shape, jnp.bfloat16),
+        in_specs=[
+            pl.BlockSpec(memory_space=pltpu.VMEM), pl.BlockSpec(memory_space=pltpu.SMEM)
+        ],
+        out_specs=pl.BlockSpec(memory_space=pltpu.VMEM),
+        compiler_params=pltpu.CompilerParams(vmem_limit_bytes=60 * 1024 * 1024),
+    )(attended, head_order)
 
 
 def solution(mesh):

time: 32.4 us -> 30.5 us (0.941)
  local copies, waits for them, and re-layouts: 1.82 us -> 0 us
    unnamed x1 -> x0, local copies, waits for them, and re-layouts: 1.82 us -> none
    pallas_call x1 -> x2, Pallas kernels: 30.4 us -> 30.4 us  [the longest x1 28.5 us: planes_local(): pl.pallas_call(plane_kernel, out_shape=jax.ShapeDtypeStruct((H, tokens, H...]
where the time goes in v8:
time: 30.5 us; the launch traced here: 30.4 us
  Pallas kernels  30.4 us (100%)
    pallas_call x1, Pallas kernels, planes_local(): pl.pallas_call(plane_kernel, out_shape=jax.ShapeDtypeStruct((H, tokens, H...  28.5 us
    pallas_call x1, Pallas kernels, planes_local(): pl.pallas_call(order_kernel, out_shape=jax.ShapeDtypeStruct(queries.shape...  1.89 us

profile of v8, /device:TPU:25, one launch (start us, length us, event | category | flops | bytes accessed | tf_op | source)
XLA Modules:
  0.0 30.4 jit_solution(3625726587287596480)
XLA Ops:
  0.0 28.5 %shard_map.55.done = bf16[28,64,128]{2,1,0:T(8,128)(2,1)} custom-call(bf16[64,3584]{1,0:T(8,128)(2,1)} %q_ref.1, bf16[64,512]{1,0:T(8,128)(2,1)} %k_ref.1, bf16[64,512]{1,0:T(8,128)(2,1)} %v_ref.1, s32[16,16,28]{2,1,0:T(8,128)} %bitcast.1), custom_call_target="tpu_custom_call" | custom-call | tf_op jit(solution)/shard_map/pallas_call | solution.py:498
  28.5 1.9 %shard_map.56 = bf16[64,3584]{1,0:T(8,128)(2,1)} custom-call(bf16[28,64,128]{2,1,0:T(8,128)(2,1)} %shard_map.55.done, s32[28]{0:T(128)} %order_ref.1), custom_call_target="tpu_custom_call" | custom-call | tf_op jit(solution)/shard_map/pallas_call | solution.py:528
